TPU v7x, 32 devices: a whole 2x2x4 slice. The times are simulated.
32 devices in a mesh: groups: 2 (over x), row: 16 (over z, y, core).
Axes of the slice: x: 2, y: 2, z: 4, core: 2. Of those that a mesh axis runs over, the one named last changes fastest.
Arguments:
- weight: bfloat16 [106496, 8192], P(('groups', 'row')), parts along dimension 0, may hold values from -18 to 18
- test_matrix: bfloat16 [53248, 240], P('row'), may hold values from -6 to 6
- rank_mask: int32 [480], P('groups'), parts along dimension 0, may hold values from 0 to 1, as said below
Outputs:
- left_factor: float32 [16384, 224], P(('groups', 'row')), parts along dimension 0
- right_factor: bfloat16 [106496, 224], P(('groups', 'row')), parts along dimension 0
- spread: float32 [2], P('groups'), parts along dimension 0
There are 2 independent parts, one for each index of `groups`. A program takes and returns all parts, laid end to end along the dimension named above; an argument that names none is the same for every part. Nothing has to cross between parts.
Inputs may be any that keep to these rules, and one draw needn't show every extreme that they name: `rank_mask`: exactly 224 entries are 1, the others 0.
All inputs are finite; a program needn't handle non-finite values.
Results may differ from a plain program's by a relative error of at most 0.0055.
Values may be sent and summed in bfloat16 or wider, within the bound.
No kernel may reach another device: no remote copies, remote signals or barrier semaphores. Data moves between devices by JAX's collectives and lax.ppermute only.
A program may use at most 192 MiB of HBM per device.

v0:
```python
import math

import jax
import jax.numpy as jnp
from jax import lax
from jax.sharding import PartitionSpec as P

RANK = 224


def selector(rank_mask, kept):
    positions = jnp.cumsum(rank_mask) - 1
    targets = lax.iota(jnp.int32, kept)
    matches = (rank_mask[:, None] == 1) & (positions[:, None] == targets[None, :])
    return matches.astype(jnp.float32)


def body(weight, test_matrix, rank_mask):
    across = (((0,), (0,)), ((), ()))
    members = lax.axis_size("row")
    picker = selector(rank_mask, RANK)
    columns = weight
    sketch_part = lax.psum_scatter(
        lax.dot_general(columns, test_matrix, across, preferred_element_type=jnp.float32),
        "row",
        scatter_dimension=0,
        tiled=True,
    ).astype(jnp.bfloat16)

    def add_rows(piece_rows):
        return jnp.dot(weight, piece_rows, preferred_element_type=jnp.float32)

    mixed = add_rows(lax.all_gather(sketch_part, "row", axis=0, tiled=True)).astype(jnp.bfloat16)
    columns = weight
    powered = lax.psum_scatter(
        lax.dot_general(columns, mixed, across, preferred_element_type=jnp.float32),
        "row",
        scatter_dimension=0,
        tiled=True,
    )
    local_gram = lax.dot_general(powered, powered, across, precision=lax.Precision.HIGHEST)
    gram_matrix = lax.psum(local_gram, "row")
    cholesky_factor = jnp.linalg.cholesky(gram_matrix)
    ortho_basis = lax.linalg.triangular_solve(
        cholesky_factor, powered, left_side=False, lower=True, transpose_a=True
    )
    own_chosen = jnp.dot(ortho_basis, picker, precision=lax.Precision.HIGHEST)
    projected = add_rows(lax.all_gather(own_chosen.astype(jnp.bfloat16), "row", axis=0, tiled=True))
    left_factor = own_chosen * math.sqrt(weight.shape[1])
    energy = lax.psum(jnp.sum(projected * projected), "row")
    spread = jnp.sqrt(energy / (weight.shape[0] * members * RANK) + 1e-06)
    right_factor = (projected / spread).astype(jnp.bfloat16)
    return (left_factor, right_factor, spread.reshape(1))


def solution(mesh):
    in_specs = (P(("groups", "row"), None), P("row", None), P("groups"))
    out_specs = (P(("groups", "row"), None), P(("groups", "row"), None), P("groups"))
    return jax.shard_map(body, mesh=mesh, in_specs=in_specs, out_specs=out_specs, check_vma=False)
```

profile of v0, /device:TPU:1, one launch (start us, length us, event | category | flops | bytes accessed | tf_op | source)
XLA Modules:
  0.0 607.0 jit_solution(12455139369986900993)
XLA Ops:
  7.2 0.0 copy-start
  7.2 0.0 reduce-scatter.3.cloned.1.call-start
  7.2 1.4 copy-done
  8.6 26.2 %fusion.20 = f32[8192,240]{1,0:T(8,128)} fusion(bf16[3328,8192]{1,0:T(8,128)(2,1)} %param.3, bf16[3328,240]{0,1:T(8,128)(2,1)S(1)} %copy-done), kind=kOutput, calls=%fused_computation.53 | convolution fusion | flops 13086228480 | bytes 63987712 | tf_op jit(solution)/shard_map/dot_general | solution.py:24
  34.8 0.0 reduce-scatter.3.cloned.1.call-update
  34.9 0.0 all-gather.3.cloned.1.call-start
  34.9 106.8 %reduce-scatter.3.cloned.1.call-done = f32[512,240]{1,0:T(8,128)} async-done(((f32[8192,240]{1,0:T(8,128)}), f32[512,240]{1,0:T(8,128)}) %reduce-scatter.3.cloned.1.call-update) | async-done | bytes 491536 | tf_op jit(solution)/shard_map/reduce_scatter | solution.py:23
  141.7 1.8 convert_element_type.17
  143.5 0.0 all-gather.3.cloned.1.call-update
  143.5 0.0 reduce-scatter.5.cloned.1.call-start
  143.6 51.8 %all-gather.3.cloned.1.call-done = bf16[8192,240]{1,0:T(8,128)(2,1)} async-done(((bf16[512,240]{1,0:T(8,128)(2,1)}), bf16[8192,240]{1,0:T(8,128)(2,1)}) %all-gather.3.cloned.1.call-update) | async-done | bytes 3932176 | tf_op jit(solution)/shard_map/all_gather | solution.py:33
  195.4 22.4 %convolution_convert_fusion.clone.4 = bf16[240,3328]{1,0:T(8,128)(2,1)S(1)} fusion(bf16[8192,240]{1,0:T(8,128)(2,1)} %all-gather.3.cloned.1.call-done, bf16[3328,8192]{1,0:T(8,128)(2,1)} %param.3), kind=kOutput, calls=%fused_computation.1.clone.clone.clone.1 | convolution fusion | flops 13087027200 | bytes 60055552 | tf_op jit(solution)/shard_map/dot_general | solution.py:31
  217.8 25.2 %convolution_bitcast_fusion = f32[8192,240]{0,1:T(8,128)} fusion(bf16[3328,8192]{1,0:T(8,128)(2,1)} %param.3, bf16[240,3328]{1,0:T(8,128)(2,1)S(1)} %convolution_convert_fusion.clone.4), kind=kOutput, calls=%fused_computation | convolution fusion | flops 13086228480 | bytes 63987712 | tf_op jit(solution)/shard_map/dot_general | solution.py:36
  243.0 0.0 copy-start.3
  243.0 0.0 reduce-scatter.5.cloned.1.call-update
  243.0 0.2 all-reduce.6.cloned.1.call-start
  243.2 0.4 copy-done.3
  243.7 0.3 reduce-window.9
  244.0 0.1 slice.54
  244.1 0.1 slice_reduce_fusion
  244.2 0.1 add_bitcast_fusion
  244.3 92.0 %reduce-scatter.5.cloned.1.call-done = f32[512,240]{0,1:T(8,128)} async-done(((f32[8192,240]{0,1:T(8,128)}), f32[512,240]{0,1:T(8,128)}) %reduce-scatter.5.cloned.1.call-update) | async-done | bytes 491536 | tf_op jit(solution)/shard_map/reduce_scatter | solution.py:35
  336.3 0.0 copy-start.2
  336.3 2.5 fusion.21
  338.8 0.0 all-reduce.6.cloned.1.call-update
  338.8 0.0 all-gather.5.cloned.1.call-start
  338.9 90.0 %all-reduce.6.cloned.1.call-done = f32[240,240]{0,1:T(8,128)} async-done(((f32[240,240]{0,1:T(8,128)}), f32[240,240]{0,1:T(8,128)}) %all-reduce.6.cloned.1.call-update) | async-done | bytes 230416 | tf_op jit(solution)/shard_map/psum | solution.py:42
  428.9 1.1 copy.9
  430.0 1.0 fusion.7
  431.0 11.7 %cholesky.51 = f32[128,128]{1,0:T(8,128)S(1)} custom-call(f32[128,128]{1,0:T(8,128)S(1)} %cholesky.124), custom_call_target="Cholesky" | custom-call | tf_op jit(solution)/shard_map/jit(cholesky)/cholesky | solution.py:43
  442.7 9.8 %custom-call.14 = f32[1,128,128]{1,2,0:T(8,128)S(1)} custom-call(f32[1,128,128]{2,1,0:T(8,128)S(1)} %get-tuple-element.26), custom_call_target="InvertDiagBlocksLowerTriangular" | custom-call | tf_op jit(solution)/shard_map/jit(cholesky)/cholesky | solution.py:43
  452.5 0.2 constant_dynamic-update-slice_fusion.1
  452.8 0.2 convolution_subtract_fusion.1
  453.0 10.2 %cholesky.110 = f32[112,112]{1,0:T(8,128)S(1)} custom-call(f32[112,112]{1,0:T(8,128)S(1)} %convolution_subtract_fusion.1), custom_call_target="Cholesky" | custom-call | tf_op jit(solution)/shard_map/jit(cholesky)/cholesky | solution.py:43
  463.3 0.6 compare_reduce_fusion
  463.9 0.6 compare_reduce_fusion.1
  465.9 0.1 fusion.12
  466.0 19.9 %custom-call.15 = f32[2,128,128]{1,2,0:T(8,128)S(1)} custom-call(f32[2,128,128]{2,1,0:T(8,128)S(1)} %pad_maximum_fusion), custom_call_target="InvertDiagBlocksLowerTriangular" | custom-call | tf_op jit(solution)/shard_map/triangular_solve | solution.py:44
  485.9 0.0 copy-done.2
  485.9 0.4 fusion.5
  486.4 0.4 convolution_subtract_fusion
  486.7 0.4 fusion.15
  487.1 1.4 fusion.19
  488.5 0.0 all-gather.5.cloned.1.call-update
  488.5 51.0 %all-gather.5.cloned.1.call-done = bf16[8192,224]{0,1:T(8,128)(2,1)} async-done(((bf16[512,224]{0,1:T(8,128)(2,1)}), bf16[8192,224]{0,1:T(8,128)(2,1)}) %all-gather.5.cloned.1.call-update) | async-done | bytes 3670032 | tf_op jit(solution)/shard_map/all_gather | solution.py:48
  539.5 0.0 copy-start.1
  539.5 26.3 %multiply_reduce_fusion = (f32[]{:T(128)}, f32[224,3328]{1,0:T(8,128)}) fusion(bf16[8192,224]{0,1:T(8,128)(2,1)} %all-gather.5.cloned.1.call-done, bf16[3328,8192]{1,0:T(8,128)(2,1)} %param.3), kind=kOutput, calls=%fused_computation.3 | convolution fusion | flops 12215304192 | bytes 61177860 | tf_op jit(solution)/shard_map/dot_general | solution.py:31
  565.8 29.7 %psum.15 = f32[]{:T(128)} all-reduce(f32[]{:T(128)} %get-tuple-element.31), channel_id=1, replica_groups=mesh['groups'=2,'row'=16] {'row'}, use_global_device_ids=true, to_apply=%region_10.11 | all-reduce | flops 1 | bytes 8 | tf_op jit(solution)/shard_map/psum | solution.py:50
  596.2 3.1 fusion
  599.3 0.0 copy-done.1
  (13 shorter events, 0.2 us)
Async XLA Ops:
  7.2 1.4 copy-start
  7.2 134.6 %reduce-scatter.3.cloned.1.call-start = ((), (), s32[]{:S(2)}) async-start(), calls=%async_computation.2 | async-start | bytes 8912896 | tf_op jit(solution)/shard_map/reduce_scatter | solution.py:23
  34.9 160.5 %all-gather.3.cloned.1.call-start = ((), (), s32[]{:S(2)}) async-start(), calls=%async_computation.3 | async-start | bytes 4456448 | tf_op jit(solution)/shard_map/all_gather | solution.py:33
  143.5 192.8 %reduce-scatter.5.cloned.1.call-start = ((), (), s32[]{:S(2)}) async-start(), calls=%async_computation.4 | async-start | bytes 8355840 | tf_op jit(solution)/shard_map/reduce_scatter | solution.py:35
  243.0 0.7 copy-start.3
  243.0 185.9 %all-reduce.6.cloned.1.call-start = ((), (), s32[]{:S(2)}) async-start(), calls=%async_computation.5 | async-start | bytes 491520 | tf_op jit(solution)/shard_map/psum | solution.py:42
  336.3 149.6 %copy-start.2 = (f32[512,240]{0,1:T(8,128)S(1)}, f32[512,240]{0,1:T(8,128)}, u32[]{:S(2)}) copy-start(f32[512,240]{0,1:T(8,128)} %reduce-scatter.5.cloned.1.call-done) | copy-start | bytes 1474564
  338.8 200.7 %all-gather.5.cloned.1.call-start = ((), (), s32[]{:S(2)}) async-start(), calls=%async_computation.6 | async-start | bytes 3899392 | tf_op jit(solution)/shard_map/all_gather | solution.py:48
  539.5 59.8 %copy-start.1 = (bf16[3328,240]{0,1:T(8,128)(2,1)S(1)}, bf16[3328,240]{0,1:T(8,128)(2,1)}, u32[]{:S(2)}) copy-start(bf16[3328,240]{0,1:T(8,128)(2,1)} %param.4) | copy-start | bytes 4792324
Sparse Core Ops, SparseCore 0:
  35.0 106.7 reduce-scatter.2
  144.5 50.8 all-gather.2
  243.1 93.1 reduce-scatter.4
  340.1 88.7 all-reduce.5
  488.6 50.8 all-gather.4
where the time goes:
time: 610 us; the launch traced here: 607 us
  waiting for transfers between devices  392 us (64%)
  matrix products  106 us (17%)
  other arithmetic  59.5 us (10%)
  blocking collectives  29.7 us (5%)
  between operations  17.1 us (3%)
    reduce_scatter x1, waiting for transfers between devices, body(): lax.psum_scatter(lax.dot_general(columns, test_matrix, across, preferred_...  107 us
    reduce_scatter x1, waiting for transfers between devices, body(): lax.psum_scatter(lax.dot_general(columns, mixed, across, preferred_elemen...  92 us
    psum x1, waiting for transfers between devices, body(): gram_matrix = lax.psum(local_gram, 'row')  90 us
    all_gather x1, waiting for transfers between devices, body(): lax.all_gather(sketch_part, 'row', axis=0, tiled=True)  51.8 us
    all_gather x1, waiting for transfers between devices, body(): lax.all_gather(own_chosen.astype(jnp.bfloat16), 'row', axis=0, tiled=True)  51 us
    dot_general x2, matrix products, add_rows(): return jnp.dot(weight, piece_rows, preferred_element_type=jnp.float32)  48.7 us
    another operation x7, other arithmetic, body(): cholesky_factor = jnp.linalg.cholesky(gram_matrix)  33.1 us
    psum x1, blocking collectives, body(): energy = lax.psum(jnp.sum(projected * projected), 'row')  29.7 us
  transfers between devices with their start and end apart: 5, of which 5 were waited for; matrix products, arithmetic and copies ran while one was open for 0% of the time, Pallas kernels for 0%

commit v1 on v0

--- a/solution.py
+++ b/solution.py
@@ -1,11 +1,16 @@
+import functools
 import math
 
 import jax
 import jax.numpy as jnp
+import numpy as np
 from jax import lax
+from jax.experimental import pallas as pl
+from jax.experimental.pallas import tpu as pltpu
 from jax.sharding import PartitionSpec as P
 
 RANK = 224
+MIB = 1024 * 1024
 
 
 def selector(rank_mask, kept):
@@ -15,13 +20,12 @@
     return matches.astype(jnp.float32)
 
 
-def body(weight, test_matrix, rank_mask):
+def plain_body(weight, test_matrix, rank_mask):
     across = (((0,), (0,)), ((), ()))
     members = lax.axis_size("row")
     picker = selector(rank_mask, RANK)
-    columns = weight
     sketch_part = lax.psum_scatter(
-        lax.dot_general(columns, test_matrix, across, preferred_element_type=jnp.float32),
+        lax.dot_general(weight, test_matrix, across, preferred_element_type=jnp.float32),
         "row",
         scatter_dimension=0,
         tiled=True,
@@ -31,9 +35,8 @@
         return jnp.dot(weight, piece_rows, preferred_element_type=jnp.float32)
 
     mixed = add_rows(lax.all_gather(sketch_part, "row", axis=0, tiled=True)).astype(jnp.bfloat16)
-    columns = weight
     powered = lax.psum_scatter(
-        lax.dot_general(columns, mixed, across, preferred_element_type=jnp.float32),
+        lax.dot_general(weight, mixed, across, preferred_element_type=jnp.float32),
         "row",
         scatter_dimension=0,
         tiled=True,
@@ -53,6 +56,298 @@
     return (left_factor, right_factor, spread.reshape(1))
 
 
+class Ring:
+    def __init__(self, members):
+        chips = members // 2
+        order = list(range(0, chips, 2)) + list(range(chips - 1, 0, -2))
+        place = {chip: at for at, chip in enumerate(order)}
+        self.chips, self.far = chips, chips // 2
+        self.pair = [(device, device ^ 1) for device in range(members)]
+        self.ahead = []
+        for at, chip in enumerate(order):
+            self.ahead.append((2 * chip, 2 * order[(at + 1) % chips]))
+            self.ahead.append((2 * chip + 1, 2 * order[at - 1] + 1))
+
+        def halves(device, steps, core):
+            at = place[device // 2] + (steps if device % 2 == 0 else -steps)
+            chip = order[at % chips]
+            return [2 * chip + core, 2 * chip + 1 - core]
+
+        self.width, self.table = {}, []
+        for device in range(members):
+            core, row = device % 2, []
+
+            def put(name, values):
+                self.width[name] = (len(row), len(values))
+                row.extend(values)
+
+            for k in range(self.far + 1):
+                one = k == self.far
+                mine, other = halves(device, k, core), halves(device, -k, 1 - core)
+                put(("sum", k), mine if k == 0 else (mine[:1] + other[:1] if one else mine + other))
+                mine, other = halves(device, -k, core), halves(device, k, 1 - core)
+                put(("use", k), mine if k == 0 else (mine[:1] + other[:1] if one else mine + other))
+            arrival = [device // 2]
+            for k in range(1, self.far):
+                arrival += [halves(device, -k, core)[0] // 2, halves(device, k, core)[0] // 2]
+            arrival.append(halves(device, self.far, core)[0] // 2)
+            put("arrival", [arrival.index(chip) for chip in range(chips)])
+            self.table.append(row)
+
+    def row(self):
+        table = jnp.asarray(np.array(self.table, np.int32))
+        row = lax.dynamic_index_in_dim(table, lax.axis_index("row"), 0, keepdims=False)
+        return {name: row[at : at + size] for name, (at, size) in self.width.items()}
+
+
+def columns_kernel(kept, ids_ref, left_ref, weight_ref, keep_ref, *give):
+    step = pl.program_id(0)
+    part = jnp.dot(left_ref[...], weight_ref[...], preferred_element_type=jnp.float32)
+    if not give:
+        keep_ref[...] = part
+        return
+
+    @pl.when(step < kept)
+    def _():
+        keep_ref[...] = part
+
+    @pl.when(step >= kept)
+    def _():
+        give[0][...] = part.astype(jnp.bfloat16)
+
+
+def column_sums(left, weight, halves, half, split):
+    rows, wide = left.shape[1], left.shape[0]
+    block = min(256, half)
+    per = half // block
+    ids = (halves[:, None] * per + jnp.arange(per, dtype=jnp.int32)[None, :]).reshape(-1)
+    steps = ids.shape[0]
+    kept = steps // 2 if split else steps
+    out_shape = [jax.ShapeDtypeStruct((wide, kept * block), jnp.float32)]
+    out_specs = [pl.BlockSpec((wide, block), lambda j, ids: (0, jnp.minimum(j, kept - 1)))]
+    if split:
+        out_shape.append(jax.ShapeDtypeStruct((wide, kept * block), jnp.bfloat16))
+        out_specs.append(pl.BlockSpec((wide, block), lambda j, ids: (0, jnp.maximum(j - kept, 0))))
+    return pl.pallas_call(
+        functools.partial(columns_kernel, kept),
+        out_shape=out_shape,
+        grid_spec=pltpu.PrefetchScalarGridSpec(
+            num_scalar_prefetch=1,
+            grid=(steps,),
+            in_specs=[
+                pl.BlockSpec((wide, rows), lambda j, ids: (0, 0)),
+                pl.BlockSpec((rows, block), lambda j, ids: (0, ids[j])),
+            ],
+            out_specs=out_specs,
+        ),
+        compiler_params=pltpu.CompilerParams(
+            dimension_semantics=("arbitrary",), vmem_limit_bytes=32 * MIB
+        ),
+        cost_estimate=pl.CostEstimate(
+            flops=2 * wide * rows * steps * block,
+            bytes_accessed=2 * rows * steps * block + 2 * rows * wide,
+            transcendentals=0,
+        ),
+    )(ids, left, weight)
+
+
+def rows_kernel(pieces, halves, chained, turned, with_gram, *refs):
+    refs = list(refs[1:])
+    weight_ref = refs.pop(0)
+    piece_refs = [refs.pop(0) for _ in range(pieces)]
+    before_ref = refs.pop(0) if chained else None
+    out_ref = refs.pop(0)
+    gram_ref = refs.pop(0) if with_gram else None
+    total_ref = refs.pop(0) if turned else out_ref
+    block, step = pl.program_id(0), pl.program_id(1)
+    steps = pieces * halves
+    piece = piece_refs[0][...]
+    if pieces == 2:
+        piece = jnp.where(step < halves, piece, piece_refs[1][...])
+    onto = (((1,), (1,)), ((), ()))
+    part = lax.dot_general(weight_ref[...], piece, onto, preferred_element_type=jnp.float32)
+
+    @pl.when(step == 0)
+    def _():
+        total_ref[...] = before_ref[...] + part if chained else part
+
+    @pl.when(step > 0)
+    def _():
+        total_ref[...] += part
+
+    if turned:
+
+        @pl.when(step == steps - 1)
+        def _():
+            out_ref[...] = total_ref[...].T.astype(jnp.bfloat16)
+
+    if with_gram:
+        slots = gram_ref.shape[0]
+        run = steps // slots
+
+        @pl.when(block == 0)
+        def _():
+            square = lax.dot_general(piece, piece, onto, preferred_element_type=jnp.float32)
+            slot = step // run
+
+            @pl.when(step % run == 0)
+            def _():
+                gram_ref[slot] = square
+
+            @pl.when(step % run > 0)
+            def _():
+                gram_ref[slot] += square
+
+
+def row_products(weight, pieces, ids, half, before, turned, with_gram):
+    rows, wide = weight.shape[0], pieces[0].shape[0]
+    halves = pieces[0].shape[1] // half
+    steps = len(pieces) * halves
+    tall = rows // 2 if rows % 256 == 0 else rows
+
+    def piece_spec(at):
+        low = at * halves
+        return pl.BlockSpec((wide, half), lambda i, j, ids: (0, jnp.clip(j - low, 0, halves - 1)))
+
+    in_specs = [pl.BlockSpec((tall, half), lambda i, j, ids: (i, ids[j]))]
+    in_specs += [piece_spec(at) for at in range(len(pieces))]
+    operands = [weight, *pieces]
+    if before is not None:
+        in_specs.append(pl.BlockSpec((tall, wide), lambda i, j, ids: (i, 0)))
+        operands.append(before)
+    if turned:
+        out_shape = [jax.ShapeDtypeStruct((wide, rows), jnp.bfloat16)]
+        out_specs = [pl.BlockSpec((wide, tall), lambda i, j, ids: (0, i))]
+    else:
+        out_shape = [jax.ShapeDtypeStruct((rows, wide), jnp.float32)]
+        out_specs = [pl.BlockSpec((tall, wide), lambda i, j, ids: (i, 0))]
+    if with_gram:
+        slots = max(1, steps // 2)
+        out_shape.append(jax.ShapeDtypeStruct((slots, wide, wide), jnp.float32))
+        out_specs.append(pl.BlockSpec((slots, wide, wide), lambda i, j, ids: (0, 0, 0)))
+    return pl.pallas_call(
+        functools.partial(rows_kernel, len(pieces), halves, before is not None, turned, with_gram),
+        out_shape=out_shape,
+        grid_spec=pltpu.PrefetchScalarGridSpec(
+            num_scalar_prefetch=1,
+            grid=(rows // tall, steps),
+            in_specs=in_specs,
+            out_specs=out_specs,
+            scratch_shapes=[pltpu.VMEM((tall, wide), jnp.float32)] if turned else [],
+        ),
+        input_output_aliases={len(operands): 0} if before is not None and not turned else {},
+        compiler_params=pltpu.CompilerParams(
+            dimension_semantics=("arbitrary", "arbitrary"), vmem_limit_bytes=40 * MIB
+        ),
+        cost_estimate=pl.CostEstimate(
+            flops=2 * rows * wide * steps * half,
+            bytes_accessed=2 * rows * steps * half + 8 * rows * wide,
+            transcendentals=0,
+        ),
+    )(ids, *operands)
+
+
+def ring_sum(ring, ids, left, weight, half):
+    got = None
+    for k in range(ring.far, 0, -1):
+        keep, give = column_sums(left, weight, ids["sum", k], half, True)
+        total = keep + lax.ppermute(give, "row", ring.pair).astype(jnp.float32)
+        if got is not None:
+            got = got.astype(jnp.float32)
+            size = got.shape[1]
+            if size < total.shape[1]:
+                total = jnp.concatenate([total[:, :size] + got, total[:, size:]], 1)
+            else:
+                total = total + got
+        got = lax.ppermute(total.astype(jnp.bfloat16), "row", ring.ahead)
+    (keep,) = column_sums(left, weight, ids["sum", 0], half, False)
+    mine = keep + got.astype(jnp.float32)
+    other = lax.ppermute(mine, "row", ring.pair)
+    return mine + jnp.concatenate([other[:, half:], other[:, :half]], 1)
+
+
+def ring_apply(ring, ids, chunk, weight, half, turned, with_gram):
+    grams, before = [], None
+    moving = chunk
+    for k in range(ring.far + 1):
+        if k == 0:
+            pieces = [chunk]
+        else:
+            moving = lax.ppermute(moving if k < ring.far else moving[:, :half], "row", ring.ahead)
+            pieces = [moving, lax.ppermute(moving, "row", ring.pair)]
+        last = k == ring.far
+        before, *gram = row_products(
+            weight, pieces, ids["use", k], half, before, turned and last, with_gram
+        )
+        grams += gram
+    return before, grams
+
+
+def group_sum(value, ring):
+    rows = value.shape[0] // 2
+    first = lax.axis_index("row") % 2 == 0
+    low, high = value[:rows], value[rows:]
+    part = jnp.where(first, low, high)
+    part = part + lax.ppermute(jnp.where(first, high, low), "row", ring.pair)
+    hop = 2
+    while hop < 2 * ring.chips:
+        swap = [(device, device ^ hop) for device in range(2 * ring.chips)]
+        part = part + lax.ppermute(part, "row", swap)
+        hop *= 2
+    other = lax.ppermute(part, "row", ring.pair)
+    return jnp.concatenate([jnp.where(first, part, other), jnp.where(first, other, part)], 0)
+
+
+def ring_body(ring, weight, test_matrix, rank_mask):
+    highest = lax.Precision.HIGHEST
+    rows, features = weight.shape
+    half = features // (2 * ring.chips)
+    ids = ring.row()
+    picker = selector(rank_mask, RANK)
+    sketch = ring_sum(ring, ids, test_matrix.T, weight, half).astype(jnp.bfloat16)
+    mixed, _ = ring_apply(ring, ids, sketch, weight, half, True, False)
+    powered = ring_sum(ring, ids, mixed, weight, half)
+    image, grams = ring_apply(
+        ring, ids, powered.astype(jnp.bfloat16), weight, half, False, True
+    )
+    image_b = image.astype(jnp.bfloat16)
+    square = lax.dot_general(
+        image_b, image_b, (((0,), (0,)), ((), ())), preferred_element_type=jnp.float32
+    )
+    square = group_sum(square, ring)
+    stack = jnp.concatenate(grams, 0)
+    gram_matrix = sum(
+        lax.dynamic_index_in_dim(stack, ids["arrival"][chip], 0, keepdims=False)
+        for chip in range(ring.chips)
+    )
+    cholesky_factor = jnp.linalg.cholesky(gram_matrix)
+    inverse = lax.linalg.triangular_solve(
+        cholesky_factor,
+        jnp.eye(gram_matrix.shape[0], dtype=jnp.float32),
+        left_side=False,
+        lower=True,
+        transpose_a=True,
+    )
+    change = jnp.dot(inverse, picker, precision=highest)
+    own = powered[:, :half]
+    left_factor = lax.dot_general(
+        own, change, (((0,), (0,)), ((), ())), precision=highest
+    ) * math.sqrt(features)
+    energy = jnp.sum(square * jnp.dot(change, change.T, precision=highest))
+    spread = jnp.sqrt(energy / (rows * 2 * ring.chips * RANK) + 1e-06)
+    right_factor = (jnp.dot(image, change, precision=highest) / spread).astype(jnp.bfloat16)
+    return (left_factor, right_factor, spread.reshape(1))
+
+
+def body(weight, test_matrix, rank_mask):
+    members = lax.axis_size("row")
+    chips = members // 2
+    paired = members % 2 == 0 and chips > 2 and chips & (chips - 1) == 0
+    if not paired or weight.shape[1] % (members * 128):
+        return plain_body(weight, test_matrix, rank_mask)
+    return ring_body(Ring(members), weight, test_matrix, rank_mask)
+
+
 def solution(mesh):
     in_specs = (P(("groups", "row"), None), P("row", None), P("groups"))
     out_specs = (P(("groups", "row"), None), P(("groups", "row"), None), P("groups"))

time: 610 us -> 430 us (0.70)
  waiting for transfers between devices: 392 us -> 61.5 us
  Pallas kernels: 0 us -> 180 us
  matrix products: 106 us -> 15.1 us
  starting transfers between devices: 0.39 us -> 34.7 us
  local copies, waits for them, and re-layouts: 3.09 us -> 35.5 us
  blocking collectives: 29.7 us -> 0 us
  other arithmetic: 59.5 us -> 74.9 us
    reduce_scatter x2 -> x0, waiting for transfers between devices: 199 us -> none  [the longest x1 107 us: body(): lax.psum_scatter(lax.dot_general(columns, test_matrix, across, preferred_...]
    pallas_call x0 -> x20, Pallas kernels: none -> 180 us  [the longest x10 96.5 us: row_products(): pl.pallas_call(functools.partial(rows_kernel, len(pieces), halves, before...]
    all_gather x2 -> x0, waiting for transfers between devices: 103 us -> none  [the longest x1 51.8 us: body(): lax.all_gather(sketch_part, 'row', axis=0, tiled=True)]
    dot_general x6 -> x5, matrix products: 104 us -> 9.14 us  [the longest x1 5.42 us: ring_body(): jnp.dot(image, change, precision=highest) / spread]
    psum x1 -> x0, waiting for transfers between devices: 90 us -> none  [body(): gram_matrix = lax.psum(local_gram, 'row')]
    ppermute x0 -> x39, waiting for transfers between devices: none -> 61.5 us  [the longest x8 26.4 us: ring_sum(): got = lax.ppermute(total.astype(jnp.bfloat16), 'row', ring.ahead)]
    ppermute x0 -> x39, starting transfers between devices: none -> 34.7 us  [the longest x8 9.04 us: ring_apply(): pieces = [moving, lax.ppermute(moving, 'row', ring.pair)]]
    psum x1 -> x0, blocking collectives: 29.7 us -> none  [body(): energy = lax.psum(jnp.sum(projected * projected), 'row')]
  transfers between devices with their start and end apart: 5 -> 39, of which waited for: 5 -> 15; matrix products, arithmetic and copies ran while one was open for 0% -> 12% of each run, Pallas kernels for 0% -> 33%
where the time goes in v1:
time: 430 us; the launch traced here: 422 us
  Pallas kernels  180 us (42%)
  other arithmetic  74.9 us (17%)
  waiting for transfers between devices  61.5 us (14%)
  local copies, waits for them, and re-layouts  35.5 us (8%)
  starting transfers between devices  34.7 us (8%)
  between operations  20.2 us (5%)
  matrix products  15.1 us (4%)
    pallas_call x10, Pallas kernels, row_products(): pl.pallas_call(functools.partial(rows_kernel, len(pieces), halves, before...  96.5 us
    pallas_call x10, Pallas kernels, column_sums(): pl.pallas_call(functools.partial(columns_kernel, kept), out_shape=out_sha...  83 us
    another operation x7, other arithmetic, ring_body(): cholesky_factor = jnp.linalg.cholesky(gram_matrix)  37.4 us
    ppermute x8, waiting for transfers between devices, ring_sum(): got = lax.ppermute(total.astype(jnp.bfloat16), 'row', ring.ahead)  26.4 us
    another operation x6, other arithmetic, ring_body(): lax.linalg.triangular_solve(cholesky_factor, jnp.eye(gram_matrix.shape[0]...  23.1 us
    ppermute x8, waiting for transfers between devices, ring_apply(): lax.ppermute(moving if k < ring.far else moving[:, :half], 'row', ring.ah...  21.3 us
    unnamed x68, local copies, waits for them, and re-layouts  17.3 us
    pallas_call x5, local copies, waits for them, and re-layouts, row_products(): pl.pallas_call(functools.partial(rows_kernel, len(pieces), halves, before...  9.56 us
  transfers between devices with their start and end apart: 39, of which 15 were waited for; matrix products, arithmetic and copies ran while one was open for 12% of the time, Pallas kernels for 33%

profile of v1, /device:TPU:1, one launch (start us, length us, event | category | flops | bytes accessed | tf_op | source)
XLA Modules:
  0.0 421.5 jit_solution(1096765518372474725)
XLA Ops:
  3.0 10.6 %shard_map.70 = (f32[240,1024]{1,0:T(8,128)S(1)}, bf16[240,1024]{1,0:T(8,128)(2,1)}) custom-call(s32[8]{0:T(128)S(1)} %add.294.ids_ref, bf16[240,3328]{1,0:T(8,128)(2,1)S(1)} %bitcast.67, bf16[3328,8192]{1,0:T(8,128)(2,1)} %refs_1_.19), custom_call_target="tpu_custom_call" | custom-call | flops 3271557120 | bytes 15228928 | tf_op jit(solution)/shard_map/pallas_call | solution.py:131
  14.9 5.5 %shard_map.71 = (f32[240,512]{1,0:T(8,128)S(1)}, bf16[240,512]{1,0:T(8,128)(2,1)S(1)}) custom-call(s32[4]{0:T(128)S(1)} %add.299.ids_ref, bf16[240,3328]{1,0:T(8,128)(2,1)S(1)} %bitcast.68, bf16[3328,8192]{1,0:T(8,128)(2,1)} %refs_1_.19), custom_call_target="tpu_custom_call" | custom-call | flops 1635778560 | bytes 8413184 | tf_op jit(solution)/shard_map/pallas_call | solution.py:131
  21.0 10.6 %shard_map.69 = (f32[240,1024]{1,0:T(8,128)S(1)}, bf16[240,1024]{1,0:T(8,128)(2,1)}) custom-call(s32[8]{0:T(128)S(1)} %add.289.ids_ref, bf16[240,3328]{1,0:T(8,128)(2,1)S(1)} %bitcast.69, bf16[3328,8192]{1,0:T(8,128)(2,1)} %refs_1_.19), custom_call_target="tpu_custom_call" | custom-call | flops 3271557120 | bytes 15228928 | tf_op jit(solution)/shard_map/pallas_call | solution.py:131
  32.7 2.7 collective-permute-start.4
  36.6 2.7 collective-permute-done.4
  41.9 9.9 %shard_map.68 = (f32[240,1024]{1,0:T(8,128)S(1)}, bf16[240,1024]{1,0:T(8,128)(2,1)S(1)}) custom-call(s32[8]{0:T(128)S(1)} %add.284.ids_ref, bf16[240,3328]{1,0:T(8,128)(2,1)S(1)} %bitcast.70, bf16[3328,8192]{1,0:T(8,128)(2,1)} %refs_1_.19), custom_call_target="tpu_custom_call" | custom-call | flops 3271557120 | bytes 15228928 | tf_op jit(solution)/shard_map/pallas_call | solution.py:131
  53.1 1.4 add_convert_fusion.3
  54.7 7.9 %collective-permute-done.6 = bf16[240,1024]{1,0:T(8,128)(2,1)S(1)} collective-permute-done((bf16[240,1024]{1,0:T(8,128)(2,1)S(1)}, bf16[240,1024]{1,0:T(8,128)(2,1)S(1)}, u32[]{:S(2)}, u32[]{:S(2)}) %collective-permute-start.6) | collective-permute-done | bytes 491552 | tf_op jit(solution)/shard_map/ppermute | solution.py:262
  63.0 5.5 %shard_map.67 = f32[240,1024]{1,0:T(8,128)S(1)} custom-call(s32[4]{0:T(128)S(1)} %add.280.ids_ref, bf16[240,3328]{1,0:T(8,128)(2,1)S(1)} %bitcast.71, bf16[3328,8192]{1,0:T(8,128)(2,1)} %refs_1_.19), custom_call_target="tpu_custom_call" | custom-call | flops 1635778560 | bytes 8413184 | tf_op jit(solution)/shard_map/pallas_call | solution.py:131
  68.5 2.3 collective-permute-done.7
  71.0 1.8 collective-permute-start.8
  72.8 2.2 collective-permute-done.8
  75.8 7.4 %collective-permute-done.9.refs_2_ = bf16[240,1024]{1,0:T(8,128)(2,1)S(1)} collective-permute-done((bf16[240,1024]{1,0:T(8,128)(2,1)S(1)}, bf16[240,1024]{1,0:T(8,128)(2,1)S(1)}, u32[]{:S(2)}, u32[]{:S(2)}) %collective-permute-start.9) | collective-permute-done | bytes 491552 | tf_op jit(solution)/shard_map/ppermute | solution.py:276
  83.8 7.4 %collective-permute-done.10.refs_2_ = bf16[240,1024]{1,0:T(8,128)(2,1)S(1)} collective-permute-done((bf16[240,1024]{1,0:T(8,128)(2,1)S(1)}, bf16[240,1024]{1,0:T(8,128)(2,1)S(1)}, u32[]{:S(2)}, u32[]{:S(2)}) %collective-permute-start.10) | collective-permute-done | bytes 491552 | tf_op jit(solution)/shard_map/ppermute | solution.py:276
  91.8 3.1 collective-permute-start.16
  94.9 6.1 %shard_map.72.refs_4_ = f32[3328,240]{1,0:T(8,128)S(1)} custom-call(s32[2]{0:T(128)S(1)} %get-tuple-element.102.refs_0_, bf16[3328,8192]{1,0:T(8,128)(2,1)} %refs_1_.19, bf16[240,1024]{1,0:T(8,128)(2,1)S(1)} %fusion.3.refs_2_), custom_call_target="tpu_custom_call" | custom-call | flops 1635778560 | bytes 13205504 | tf_op jit(solution)/shard_map/pallas_call | solution.py:228
  102.1 11.3 %shard_map.73.refs_4_ = f32[3328,240]{1,0:T(8,128)S(1)} custom-call(s32[4]{0:T(128)S(1)} %get-tuple-element.95.refs_0_, bf16[3328,8192]{1,0:T(8,128)(2,1)} %refs_1_.19, bf16[240,1024]{1,0:T(8,128)(2,1)S(1)} %collective-permute-done.9.refs_2_, bf16[240,1024]{1,0:T(8,128)(2,1)S(1)} %collective-permute-done.16.refs_3_, ...), custom_call_target="tpu_custom_call", output_to_operand_aliasing={{}: (4, {})} | custom-call | flops 3271557120 | bytes 20021248 | tf_op jit(solution)/shard_map/pallas_call | solution.py:228
  114.3 11.3 %shard_map.74.refs_4_ = f32[3328,240]{1,0:T(8,128)S(1)} custom-call(s32[4]{0:T(128)S(1)} %get-tuple-element.96.refs_0_, bf16[3328,8192]{1,0:T(8,128)(2,1)} %refs_1_.19, bf16[240,1024]{1,0:T(8,128)(2,1)S(1)} %collective-permute-done.10.refs_2_, bf16[240,1024]{1,0:T(8,128)(2,1)S(1)} %collective-permute-done.15.refs_3_, ...), custom_call_target="tpu_custom_call", output_to_operand_aliasing={{}: (4, {})} | custom-call | flops 3271557120 | bytes 20021248 | tf_op jit(solution)/shard_map/pallas_call | solution.py:228
  126.7 11.4 %shard_map.75.refs_4_ = f32[3328,240]{1,0:T(8,128)S(1)} custom-call(s32[4]{0:T(128)S(1)} %get-tuple-element.97.refs_0_, bf16[3328,8192]{1,0:T(8,128)(2,1)} %refs_1_.19, bf16[240,1024]{1,0:T(8,128)(2,1)S(1)} %collective-permute-done.11.refs_2_, bf16[240,1024]{1,0:T(8,128)(2,1)S(1)} %collective-permute-done.14.refs_3_, ...), custom_call_target="tpu_custom_call", output_to_operand_aliasing={{}: (4, {})} | custom-call | flops 3271557120 | bytes 20021248 | tf_op jit(solution)/shard_map/pallas_call | solution.py:228
  138.1 6.8 %shard_map.76.left_ref = bf16[240,3328]{1,0:T(8,128)(2,1)S(1)} custom-call(s32[2]{0:T(128)S(1)} %get-tuple-element.103.refs_0_, bf16[3328,8192]{1,0:T(8,128)(2,1)} %refs_1_.19, bf16[240,512]{1,0:T(8,128)(2,1)S(1)} %collective-permute-done.12.refs_2_, bf16[240,512]{1,0:T(8,128)(2,1)S(1)} %collective-permute-done.13.refs_3_, f32[3328,240]{1,0:T(8,128)S(1)} %shard_map.75.refs_4_), custom_call_target="tpu_custom_call" | custom-call | flops 1635778560 | bytes 13205504 | tf_op jit(solution)/shard_map/pallas_call | solution.py:228
  144.9 5.5 %shard_map.81 = (f32[240,512]{1,0:T(8,128)S(1)}, bf16[240,512]{1,0:T(8,128)(2,1)S(1)}) custom-call(s32[4]{0:T(128)S(1)} %add.299.ids_ref, bf16[240,3328]{1,0:T(8,128)(2,1)S(1)} %shard_map.76.left_ref, bf16[3328,8192]{1,0:T(8,128)(2,1)} %refs_1_.19), custom_call_target="tpu_custom_call" | custom-call | flops 1635778560 | bytes 8413184 | tf_op jit(solution)/shard_map/pallas_call | solution.py:131
  150.4 10.0 %shard_map.80 = (f32[240,1024]{1,0:T(8,128)S(1)}, bf16[240,1024]{1,0:T(8,128)(2,1)S(1)}) custom-call(s32[8]{0:T(128)S(1)} %copy-done.14, bf16[240,3328]{1,0:T(8,128)(2,1)S(1)} %shard_map.76.left_ref, bf16[3328,8192]{1,0:T(8,128)(2,1)} %refs_1_.19), custom_call_target="tpu_custom_call" | custom-call | flops 3271557120 | bytes 15228928 | tf_op jit(solution)/shard_map/pallas_call | solution.py:131
  161.0 9.9 %shard_map.79 = (f32[240,1024]{1,0:T(8,128)S(1)}, bf16[240,1024]{1,0:T(8,128)(2,1)S(1)}) custom-call(s32[8]{0:T(128)S(1)} %add.289.ids_ref, bf16[240,3328]{1,0:T(8,128)(2,1)S(1)} %shard_map.76.left_ref, bf16[3328,8192]{1,0:T(8,128)(2,1)} %refs_1_.19), custom_call_target="tpu_custom_call" | custom-call | flops 3271557120 | bytes 15228928 | tf_op jit(solution)/shard_map/pallas_call | solution.py:131
  172.1 4.4 %collective-permute-done.21 = bf16[240,512]{1,0:T(8,128)(2,1)S(1)} collective-permute-done((bf16[240,512]{1,0:T(8,128)(2,1)S(1)}, bf16[240,512]{1,0:T(8,128)(2,1)S(1)}, u32[]{:S(2)}, u32[]{:S(2)}) %collective-permute-start.21) | collective-permute-done | bytes 245792 | tf_op jit(solution)/shard_map/ppermute | solution.py:262
  177.4 10.0 %shard_map.78 = (f32[240,1024]{1,0:T(8,128)S(1)}, bf16[240,1024]{1,0:T(8,128)(2,1)S(1)}) custom-call(s32[8]{0:T(128)S(1)} %add.284.ids_ref, bf16[240,3328]{1,0:T(8,128)(2,1)S(1)} %shard_map.76.left_ref, bf16[3328,8192]{1,0:T(8,128)(2,1)} %refs_1_.19), custom_call_target="tpu_custom_call" | custom-call | flops 3271557120 | bytes 15228928 | tf_op jit(solution)/shard_map/pallas_call | solution.py:131
  187.4 2.2 collective-permute-start.17
  191.1 6.8 %collective-permute-done.23 = bf16[240,1024]{1,0:T(8,128)(2,1)S(1)} collective-permute-done((bf16[240,1024]{1,0:T(8,128)(2,1)S(1)}, bf16[240,1024]{1,0:T(8,128)(2,1)S(1)}, u32[]{:S(2)}, u32[]{:S(2)}) %collective-permute-start.23) | collective-permute-done | bytes 491552 | tf_op jit(solution)/shard_map/ppermute | solution.py:262
  198.3 5.5 %shard_map.77 = f32[240,1024]{1,0:T(8,128)S(1)} custom-call(s32[4]{0:T(128)S(1)} %add.280.ids_ref, bf16[240,3328]{1,0:T(8,128)(2,1)S(1)} %shard_map.76.left_ref, bf16[3328,8192]{1,0:T(8,128)(2,1)} %refs_1_.19), custom_call_target="tpu_custom_call" | custom-call | flops 1635778560 | bytes 8413184 | tf_op jit(solution)/shard_map/pallas_call | solution.py:131
  203.8 2.3 collective-permute-done.24
  206.2 1.8 collective-permute-start.25
  208.6 1.6 collective-permute-done.25
  213.1 6.4 %collective-permute-done.26.refs_2_ = bf16[240,1024]{1,0:T(8,128)(2,1)} collective-permute-done((bf16[240,1024]{1,0:T(8,128)(2,1)S(1)}, bf16[240,1024]{1,0:T(8,128)(2,1)}, u32[]{:S(2)}, u32[]{:S(2)}) %collective-permute-start.26) | collective-permute-done | bytes 491552 | tf_op jit(solution)/shard_map/ppermute | solution.py:276
  235.8 2.7 collective-permute-start.27
  239.8 6.5 %shard_map.82 = (f32[3328,240]{1,0:T(8,128)S(1)}, f32[1,240,240]{2,1,0:T(8,128)S(1)}) custom-call(s32[2]{0:T(128)S(1)} %copy-done.12, bf16[3328,8192]{1,0:T(8,128)(2,1)} %refs_1_.19, bf16[240,1024]{1,0:T(8,128)(2,1)S(1)} %copy-done.3), custom_call_target="tpu_custom_call" | custom-call | flops 1635778560 | bytes 13205504 | tf_op jit(solution)/shard_map/pallas_call | solution.py:228
  247.0 1.8 copy.20
  249.0 1.7 constant_dynamic-update-slice_fusion.4
  250.7 12.1 %shard_map.83 = (f32[3328,240]{1,0:T(8,128)S(1)}, f32[2,240,240]{2,1,0:T(8,128)S(1)}) custom-call(s32[4]{0:T(128)S(1)} %copy-done.22, bf16[3328,8192]{1,0:T(8,128)(2,1)} %refs_1_.19, bf16[240,1024]{1,0:T(8,128)(2,1)} %collective-permute-done.26.refs_2_, bf16[240,1024]{1,0:T(8,128)(2,1)} %collective-permute-done.27.refs_3_, ...), custom_call_target="tpu_custom_call", output_to_operand_aliasing={{0}: (4, {})} | custom-call | flops 3271557120 | bytes 20021248 | tf_op jit(solution)/shard_map/pallas_call | solution.py:228
  263.5 2.0 copy.21
  265.8 1.8 constant_dynamic-update-slice_fusion.3
  267.6 1.7 slice.254
  270.6 12.1 %shard_map.84 = (f32[3328,240]{1,0:T(8,128)S(1)}, f32[2,240,240]{2,1,0:T(8,128)S(1)}) custom-call(s32[4]{0:T(128)S(1)} %copy-done.20, bf16[3328,8192]{1,0:T(8,128)(2,1)} %refs_1_.19, bf16[240,1024]{1,0:T(8,128)(2,1)} %collective-permute-done.28.refs_2_, bf16[240,1024]{1,0:T(8,128)(2,1)} %collective-permute-done.29.refs_3_, ...), custom_call_target="tpu_custom_call", output_to_operand_aliasing={{0}: (4, {})} | custom-call | flops 3271557120 | bytes 20021248 | tf_op jit(solution)/shard_map/pallas_call | solution.py:228
  283.4 2.0 copy.22
  285.4 1.9 constant_dynamic-update-slice_fusion.2
  287.9 12.0 %shard_map.85 = (f32[3328,240]{1,0:T(8,128)S(1)}, f32[2,240,240]{2,1,0:T(8,128)S(1)}) custom-call(s32[4]{0:T(128)S(1)} %copy-done.18, bf16[3328,8192]{1,0:T(8,128)(2,1)} %refs_1_.19, bf16[240,1024]{1,0:T(8,128)(2,1)} %collective-permute-done.30.refs_2_, bf16[240,1024]{1,0:T(8,128)(2,1)} %collective-permute-done.31.refs_3_, ...), custom_call_target="tpu_custom_call", output_to_operand_aliasing={{0}: (4, {})} | custom-call | flops 3271557120 | bytes 20021248 | tf_op jit(solution)/shard_map/pallas_call | solution.py:228
  300.7 2.0 copy.23
  302.7 1.9 constant_dynamic-update-slice_fusion.1
  304.6 6.9 %shard_map.86 = (f32[3328,240]{1,0:T(8,128)S(1)}, f32[1,240,240]{2,1,0:T(8,128)S(1)}) custom-call(s32[2]{0:T(128)S(1)} %copy-done.16, bf16[3328,8192]{1,0:T(8,128)(2,1)} %refs_1_.19, bf16[240,512]{1,0:T(8,128)(2,1)} %collective-permute-done.32.refs_2_, bf16[240,512]{1,0:T(8,128)(2,1)} %collective-permute-done.33.refs_3_, ...), custom_call_target="tpu_custom_call", output_to_operand_aliasing={{0}: (4, {})} | custom-call | flops 1635778560 | bytes 13205504 | tf_op jit(solution)/shard_map/pallas_call | solution.py:228
  312.2 1.8 copy.24
  314.0 1.7 constant_dynamic-update-slice_fusion
  315.7 2.4 fusion.39
  318.1 1.8 copy.25
  319.9 1.8 fusion.12
  323.1 12.5 %cholesky.51 = f32[128,128]{1,0:T(8,128)S(1)} custom-call(f32[128,128]{1,0:T(8,128)} %cholesky.124), custom_call_target="Cholesky" | custom-call | tf_op jit(solution)/shard_map/jit(cholesky)/cholesky | solution.py:323
  337.0 10.6 %custom-call.14 = f32[1,128,128]{1,2,0:T(8,128)S(1)} custom-call(f32[1,128,128]{2,1,0:T(8,128)} %get-tuple-element.84), custom_call_target="InvertDiagBlocksLowerTriangular" | custom-call | tf_op jit(solution)/shard_map/jit(cholesky)/cholesky | solution.py:323
  347.6 1.6 constant_dynamic-update-slice_fusion.5
  350.4 10.9 %cholesky.110 = f32[112,112]{1,0:T(8,128)} custom-call(f32[112,112]{1,0:T(8,128)S(1)} %convolution_subtract_fusion.1), custom_call_target="Cholesky" | custom-call | tf_op jit(solution)/shard_map/jit(cholesky)/cholesky | solution.py:323
  361.2 1.4 select_reduce_fusion.1
  369.7 21.3 %custom-call.15 = f32[2,128,128]{1,2,0:T(8,128)} custom-call(f32[2,128,128]{2,1,0:T(8,128)} %pad_maximum_fusion.2), custom_call_target="InvertDiagBlocksLowerTriangular" | custom-call | tf_op jit(solution)/shard_map/triangular_solve | solution.py:324
  394.7 2.9 collective-permute-done.35
  399.2 2.2 collective-permute-done.36
  401.5 1.8 collective-permute-start.37
  403.8 3.7 collective-permute-done.37
  407.5 3.7 collective-permute-start.38
  414.6 5.4 %fusion = bf16[3328,224]{0,1:T(8,128)(2,1)} fusion(f32[3328,240]{1,0:T(8,128)S(1)} %get-tuple-element.54, f32[240,224]{0,1:T(8,128)} %copy-done.23, f32[]{:T(128)} %sqrt.3), kind=kOutput, calls=%fused_computation.1 | convolution fusion | flops 2148450304 | bytes 4900868 | tf_op jit(solution)/shard_map/dot_general | solution.py:338
  (187 shorter events, 50.0 us)
Async XLA Ops:
  1.3 13.3 %copy-start.29 = (s32[1,40]{1,0:T(1,128)}, s32[1,40]{1,0:T(1,128)S(1)}, u32[]{:S(2)}) copy-start(s32[1,40]{1,0:T(1,128)S(1)} %constant_dynamic-slice_fusion) | copy-start | bytes 484
  1.4 100.7 %copy-start.21 = (s32[4]{0:T(128)}, s32[4]{0:T(128)S(1)}, u32[]{:S(2)}) copy-start(s32[4]{0:T(128)S(1)} %get-tuple-element.95.refs_0_) | copy-start | bytes 52
  1.4 112.9 %copy-start.19 = (s32[4]{0:T(128)}, s32[4]{0:T(128)S(1)}, u32[]{:S(2)}) copy-start(s32[4]{0:T(128)S(1)} %get-tuple-element.96.refs_0_) | copy-start | bytes 52
  1.4 125.3 %copy-start.17 = (s32[4]{0:T(128)}, s32[4]{0:T(128)S(1)}, u32[]{:S(2)}) copy-start(s32[4]{0:T(128)S(1)} %get-tuple-element.97.refs_0_) | copy-start | bytes 52
  1.6 12.1 %copy-start.13 = (s32[8]{0:T(128)}, s32[8]{0:T(128)S(1)}, u32[]{:S(2)}) copy-start(s32[8]{0:T(128)S(1)} %add.294.ids_ref) | copy-start | bytes 100
  1.6 1.4 copy-start
  3.0 11.9 %copy-start.1 = (bf16[3328,240]{0,1:T(8,128)(2,1)S(1)}, bf16[3328,240]{0,1:T(8,128)(2,1)}, u32[]{:S(2)}) copy-start(bf16[3328,240]{0,1:T(8,128)(2,1)} %param.5) | copy-start | bytes 4792324
  13.6 0.9 copy-start.4
  14.6 20.9 %collective-permute-start.2 = (bf16[240,1024]{1,0:T(8,128)(2,1)}, bf16[240,1024]{1,0:T(8,128)(2,1)}, u32[]{:S(2)}, u32[]{:S(2)}) collective-permute-start(bf16[240,1024]{1,0:T(8,128)(2,1)} %get-tuple-element.34), channel_id=1, source_target_pairs={{0,1},{1,0},{2,3},{3,2},{4,5},{5,4},{6,7},{7,6},{8,9},{9,8},{10,11... | collective-permute-start | bytes 1474568 | tf_op jit(solution)/shard_map/ppermute | solution.py:254
  14.7 80.2 %copy-start.11 = (s32[2]{0:T(128)}, s32[2]{0:T(128)S(1)}, u32[]{:S(2)}) copy-start(s32[2]{0:T(128)S(1)} %get-tuple-element.102.refs_0_) | copy-start | bytes 28
  14.7 123.4 %copy-start.15 = (s32[2]{0:T(128)}, s32[2]{0:T(128)S(1)}, u32[]{:S(2)}) copy-start(s32[2]{0:T(128)S(1)} %get-tuple-element.103.refs_0_) | copy-start | bytes 28
  20.4 11.3 %collective-permute-start.3 = (bf16[240,512]{1,0:T(8,128)(2,1)S(1)}, bf16[240,512]{1,0:T(8,128)(2,1)}, u32[]{:S(2)}, u32[]{:S(2)}) collective-permute-start(bf16[240,512]{1,0:T(8,128)(2,1)S(1)} %get-tuple-element.36), channel_id=1, source_target_pairs={{0,1},{1,0},{2,3},{3,2},{4,5},{5,4},{6,7},{7,6},{8,9},{9,8},{10,11... | collective-permute-start | bytes 737288 | tf_op jit(solution)/shard_map/ppermute | solution.py:254
  21.0 14.4 %copy-start.5 = (f32[240,1024]{1,0:T(8,128)S(1)}, f32[240,1024]{1,0:T(8,128)}, u32[]{:S(2)}) copy-start(f32[240,1024]{1,0:T(8,128)} %copy-done.4) | copy-start | bytes 2949124
  31.6 21.5 %collective-permute-start.1 = (bf16[240,1024]{1,0:T(8,128)(2,1)}, bf16[240,1024]{1,0:T(8,128)(2,1)}, u32[]{:S(2)}, u32[]{:S(2)}) collective-permute-start(bf16[240,1024]{1,0:T(8,128)(2,1)} %get-tuple-element.32), channel_id=1, source_target_pairs={{0,1},{1,0},{2,3},{3,2},{4,5},{5,4},{6,7},{7,6},{8,9},{9,8},{10,11... | collective-permute-start | bytes 1474568 | tf_op jit(solution)/shard_map/ppermute | solution.py:254
  32.7 6.7 %collective-permute-start.4 = (bf16[240,512]{1,0:T(8,128)(2,1)S(1)}, bf16[240,512]{1,0:T(8,128)(2,1)S(1)}, u32[]{:S(2)}, u32[]{:S(2)}) collective-permute-start(bf16[240,512]{1,0:T(8,128)(2,1)S(1)} %add_convert_fusion.5), channel_id=1, source_target_pairs={{0,4},{1,3},{4,8},{5,1},{8,12},{9,5},{12,14},{13,9},{14,10},{15,13... | collective-permute-start | bytes 737288 | tf_op jit(solution)/shard_map/ppermute | solution.py:262
  40.3 12.8 %collective-permute-start.5 = (bf16[240,1024]{1,0:T(8,128)(2,1)}, bf16[240,1024]{1,0:T(8,128)(2,1)}, u32[]{:S(2)}, u32[]{:S(2)}) collective-permute-start(bf16[240,1024]{1,0:T(8,128)(2,1)} %pad_maximum_fusion), channel_id=1, source_target_pairs={{0,4},{1,3},{4,8},{5,1},{8,12},{9,5},{12,14},{13,9},{14,10},{15,13... | collective-permute-start | bytes 1474568 | tf_op jit(solution)/shard_map/ppermute | solution.py:262
  51.8 2.9 collective-permute-start
  54.5 8.0 %collective-permute-start.6 = (bf16[240,1024]{1,0:T(8,128)(2,1)S(1)}, bf16[240,1024]{1,0:T(8,128)(2,1)S(1)}, u32[]{:S(2)}, u32[]{:S(2)}) collective-permute-start(bf16[240,1024]{1,0:T(8,128)(2,1)S(1)} %add_convert_fusion.3), channel_id=1, source_target_pairs={{0,4},{1,3},{4,8},{5,1},{8,12},{9,5},{12,14},{13,9},{14,10},{15,13... | collective-permute-start | bytes 1474568 | tf_op jit(solution)/shard_map/ppermute | solution.py:262
  62.8 8.0 %collective-permute-start.7 = (bf16[240,1024]{1,0:T(8,128)(2,1)S(1)}, bf16[240,1024]{1,0:T(8,128)(2,1)S(1)}, u32[]{:S(2)}, u32[]{:S(2)}) collective-permute-start(bf16[240,1024]{1,0:T(8,128)(2,1)S(1)} %add_convert_fusion.2), channel_id=1, source_target_pairs={{0,4},{1,3},{4,8},{5,1},{8,12},{9,5},{12,14},{13,9},{14,10},{15,13... | collective-permute-start | bytes 1474568 | tf_op jit(solution)/shard_map/ppermute | solution.py:262
  71.0 4.0 collective-permute-start.8
  75.2 8.0 %collective-permute-start.9 = (bf16[240,1024]{1,0:T(8,128)(2,1)S(1)}, bf16[240,1024]{1,0:T(8,128)(2,1)S(1)}, u32[]{:S(2)}, u32[]{:S(2)}) collective-permute-start(bf16[240,1024]{1,0:T(8,128)(2,1)S(1)} %fusion.3.refs_2_), channel_id=1, source_target_pairs={{0,4},{1,3},{4,8},{5,1},{8,12},{9,5},{12,14},{13,9},{14,10},{15,13... | collective-permute-start | bytes 1474568 | tf_op jit(solution)/shard_map/ppermute | solution.py:276
  83.2 8.0 %collective-permute-start.10 = (bf16[240,1024]{1,0:T(8,128)(2,1)S(1)}, bf16[240,1024]{1,0:T(8,128)(2,1)S(1)}, u32[]{:S(2)}, u32[]{:S(2)}) collective-permute-start(bf16[240,1024]{1,0:T(8,128)(2,1)S(1)} %collective-permute-done.9.refs_2_), channel_id=1, source_target_pairs={{0,4},{1,3},{4,8},{5,1},{8,12},{9,5},{12,14},{13,9},{14,10},{15,13... | collective-permute-start | bytes 1474568 | tf_op jit(solution)/shard_map/ppermute | solution.py:276
  91.2 9.8 %collective-permute-start.11 = (bf16[240,1024]{1,0:T(8,128)(2,1)S(1)}, bf16[240,1024]{1,0:T(8,128)(2,1)S(1)}, u32[]{:S(2)}, u32[]{:S(2)}) collective-permute-start(bf16[240,1024]{1,0:T(8,128)(2,1)S(1)} %collective-permute-done.10.refs_2_), channel_id=1, source_target_pairs={{0,4},{1,3},{4,8},{5,1},{8,12},{9,5},{12,14},{13,9},{14,10},{15,13... | collective-permute-start | bytes 1474568 | tf_op jit(solution)/shard_map/ppermute | solution.py:276
  91.8 10.4 %collective-permute-start.16 = (bf16[240,1024]{1,0:T(8,128)(2,1)S(1)}, bf16[240,1024]{1,0:T(8,128)(2,1)S(1)}, u32[]{:S(2)}, u32[]{:S(2)}) collective-permute-start(bf16[240,1024]{1,0:T(8,128)(2,1)S(1)} %collective-permute-done.9.refs_2_), channel_id=1, source_target_pairs={{0,1},{1,0},{2,3},{3,2},{4,5},{5,4},{6,7},{7,6},{8,9},{9,8},{10,11... | collective-permute-start | bytes 1474568 | tf_op jit(solution)/shard_map/ppermute | solution.py:277
  94.9 19.4 %collective-permute-start.15 = (bf16[240,1024]{1,0:T(8,128)(2,1)S(1)}, bf16[240,1024]{1,0:T(8,128)(2,1)S(1)}, u32[]{:S(2)}, u32[]{:S(2)}) collective-permute-start(bf16[240,1024]{1,0:T(8,128)(2,1)S(1)} %collective-permute-done.10.refs_2_), channel_id=1, source_target_pairs={{0,1},{1,0},{2,3},{3,2},{4,5},{5,4},{6,7},{7,6},{8,9},{9,8},{10,11... | collective-permute-start | bytes 1474568 | tf_op jit(solution)/shard_map/ppermute | solution.py:277
  101.0 25.7 %collective-permute-start.14 = (bf16[240,1024]{1,0:T(8,128)(2,1)S(1)}, bf16[240,1024]{1,0:T(8,128)(2,1)S(1)}, u32[]{:S(2)}, u32[]{:S(2)}) collective-permute-start(bf16[240,1024]{1,0:T(8,128)(2,1)S(1)} %collective-permute-done.11.refs_2_), channel_id=1, source_target_pairs={{0,1},{1,0},{2,3},{3,2},{4,5},{5,4},{6,7},{7,6},{8,9},{9,8},{10,11... | collective-permute-start | bytes 1474568 | tf_op jit(solution)/shard_map/ppermute | solution.py:277
  113.5 12.2 %collective-permute-start.12 = (bf16[240,512]{1,0:T(8,128)(2,1)S(1)}, bf16[240,512]{1,0:T(8,128)(2,1)S(1)}, u32[]{:S(2)}, u32[]{:S(2)}) collective-permute-start(bf16[240,512]{1,0:T(8,128)(2,1)S(1)} %slice.248), channel_id=1, source_target_pairs={{0,4},{1,3},{4,8},{5,1},{8,12},{9,5},{12,14},{13,9},{14,10},{15,13... | collective-permute-start | bytes 737288 | tf_op jit(solution)/shard_map/ppermute | solution.py:276
  125.7 12.4 %collective-permute-start.13 = (bf16[240,512]{1,0:T(8,128)(2,1)S(1)}, bf16[240,512]{1,0:T(8,128)(2,1)S(1)}, u32[]{:S(2)}, u32[]{:S(2)}) collective-permute-start(bf16[240,512]{1,0:T(8,128)(2,1)S(1)} %collective-permute-done.12.refs_2_), channel_id=1, source_target_pairs={{0,1},{1,0},{2,3},{3,2},{4,5},{5,4},{6,7},{7,6},{8,9},{9,8},{10,11... | collective-permute-start | bytes 737288 | tf_op jit(solution)/shard_map/ppermute | solution.py:277
  144.9 5.5 %copy-start.14 = (s32[8]{0:T(128)S(1)}, s32[8]{0:T(128)}, u32[]{:S(2)}) copy-start(s32[8]{0:T(128)} %copy-done.13) | copy-start | bytes 100
  160.4 10.7 %collective-permute-start.20 = (bf16[240,512]{1,0:T(8,128)(2,1)S(1)}, bf16[240,512]{1,0:T(8,128)(2,1)S(1)}, u32[]{:S(2)}, u32[]{:S(2)}) collective-permute-start(bf16[240,512]{1,0:T(8,128)(2,1)S(1)} %get-tuple-element.44), channel_id=1, source_target_pairs={{0,1},{1,0},{2,3},{3,2},{4,5},{5,4},{6,7},{7,6},{8,9},{9,8},{10,11... | collective-permute-start | bytes 737288 | tf_op jit(solution)/shard_map/ppermute | solution.py:254
  160.5 11.4 %collective-permute-start.19 = (bf16[240,1024]{1,0:T(8,128)(2,1)S(1)}, bf16[240,1024]{1,0:T(8,128)(2,1)S(1)}, u32[]{:S(2)}, u32[]{:S(2)}) collective-permute-start(bf16[240,1024]{1,0:T(8,128)(2,1)S(1)} %get-tuple-element.42), channel_id=1, source_target_pairs={{0,1},{1,0},{2,3},{3,2},{4,5},{5,4},{6,7},{7,6},{8,9},{9,8},{10,11... | collective-permute-start | bytes 1474568 | tf_op jit(solution)/shard_map/ppermute | solution.py:254
  170.9 18.7 %collective-permute-start.18 = (bf16[240,1024]{1,0:T(8,128)(2,1)S(1)}, bf16[240,1024]{1,0:T(8,128)(2,1)S(1)}, u32[]{:S(2)}, u32[]{:S(2)}) collective-permute-start(bf16[240,1024]{1,0:T(8,128)(2,1)S(1)} %get-tuple-element.40), channel_id=1, source_target_pairs={{0,1},{1,0},{2,3},{3,2},{4,5},{5,4},{6,7},{7,6},{8,9},{9,8},{10,11... | collective-permute-start | bytes 1474568 | tf_op jit(solution)/shard_map/ppermute | solution.py:254
  171.2 5.4 %collective-permute-start.21 = (bf16[240,512]{1,0:T(8,128)(2,1)S(1)}, bf16[240,512]{1,0:T(8,128)(2,1)S(1)}, u32[]{:S(2)}, u32[]{:S(2)}) collective-permute-start(bf16[240,512]{1,0:T(8,128)(2,1)S(1)} %add_convert_fusion.4), channel_id=1, source_target_pairs={{0,4},{1,3},{4,8},{5,1},{8,12},{9,5},{12,14},{13,9},{14,10},{15,13... | collective-permute-start | bytes 737288 | tf_op jit(solution)/shard_map/ppermute | solution.py:262
  176.7 12.9 %collective-permute-start.22 = (bf16[240,1024]{1,0:T(8,128)(2,1)S(1)}, bf16[240,1024]{1,0:T(8,128)(2,1)S(1)}, u32[]{:S(2)}, u32[]{:S(2)}) collective-permute-start(bf16[240,1024]{1,0:T(8,128)(2,1)S(1)} %pad_maximum_fusion.1), channel_id=1, source_target_pairs={{0,4},{1,3},{4,8},{5,1},{8,12},{9,5},{12,14},{13,9},{14,10},{15,13... | collective-permute-start | bytes 1474568 | tf_op jit(solution)/shard_map/ppermute | solution.py:262
  187.4 3.7 collective-permute-start.17
  189.8 8.0 %collective-permute-start.23 = (bf16[240,1024]{1,0:T(8,128)(2,1)S(1)}, bf16[240,1024]{1,0:T(8,128)(2,1)S(1)}, u32[]{:S(2)}, u32[]{:S(2)}) collective-permute-start(bf16[240,1024]{1,0:T(8,128)(2,1)S(1)} %add_convert_fusion.1), channel_id=1, source_target_pairs={{0,4},{1,3},{4,8},{5,1},{8,12},{9,5},{12,14},{13,9},{14,10},{15,13... | collective-permute-start | bytes 1474568 | tf_op jit(solution)/shard_map/ppermute | solution.py:262
  198.1 8.0 %collective-permute-start.24 = (bf16[240,1024]{1,0:T(8,128)(2,1)S(1)}, bf16[240,1024]{1,0:T(8,128)(2,1)S(1)}, u32[]{:S(2)}, u32[]{:S(2)}) collective-permute-start(bf16[240,1024]{1,0:T(8,128)(2,1)S(1)} %add_convert_fusion), channel_id=1, source_target_pairs={{0,4},{1,3},{4,8},{5,1},{8,12},{9,5},{12,14},{13,9},{14,10},{15,13... | collective-permute-start | bytes 1474568 | tf_op jit(solution)/shard_map/ppermute | solution.py:262
  203.8 4.3 %copy-start.31 = (s32[240]{0:T(256)S(1)}, s32[240]{0:T(256)}, u32[]{:S(2)}) copy-start(s32[240]{0:T(256)} %param.6) | copy-start | bytes 2884
  206.2 4.0 collective-permute-start.25
  210.3 9.4 %copy-start.30 = (s32[1,40]{1,0:T(1,128)S(1)}, s32[1,40]{1,0:T(1,128)}, u32[]{:S(2)}) copy-start(s32[1,40]{1,0:T(1,128)} %copy-done.29) | copy-start | bytes 484
  210.3 28.4 %copy-start.12 = (s32[2]{0:T(128)S(1)}, s32[2]{0:T(128)}, u32[]{:S(2)}) copy-start(s32[2]{0:T(128)} %copy-done.11) | copy-start | bytes 28
  211.4 8.1 %collective-permute-start.26 = (bf16[240,1024]{1,0:T(8,128)(2,1)S(1)}, bf16[240,1024]{1,0:T(8,128)(2,1)}, u32[]{:S(2)}, u32[]{:S(2)}) collective-permute-start(bf16[240,1024]{1,0:T(8,128)(2,1)S(1)} %get-tuple-element.75.refs_2_), channel_id=1, source_target_pairs={{0,4},{1,3},{4,8},{5,1},{8,12},{9,5},{12,14},{13,9},{14,10},{15,13... | collective-permute-start | bytes 1474568 | tf_op jit(solution)/shard_map/ppermute | solution.py:276
  219.5 19.0 %collective-permute-start.28 = (bf16[240,1024]{1,0:T(8,128)(2,1)}, bf16[240,1024]{1,0:T(8,128)(2,1)}, u32[]{:S(2)}, u32[]{:S(2)}) collective-permute-start(bf16[240,1024]{1,0:T(8,128)(2,1)} %collective-permute-done.26.refs_2_), channel_id=1, source_target_pairs={{0,4},{1,3},{4,8},{5,1},{8,12},{9,5},{12,14},{13,9},{14,10},{15,13... | collective-permute-start | bytes 1474568 | tf_op jit(solution)/shard_map/ppermute | solution.py:276
  235.8 14.9 %collective-permute-start.27 = (bf16[240,1024]{1,0:T(8,128)(2,1)}, bf16[240,1024]{1,0:T(8,128)(2,1)}, u32[]{:S(2)}, u32[]{:S(2)}) collective-permute-start(bf16[240,1024]{1,0:T(8,128)(2,1)} %collective-permute-done.26.refs_2_), channel_id=1, source_target_pairs={{0,1},{1,0},{2,3},{3,2},{4,5},{5,4},{6,7},{7,6},{8,9},{9,8},{10,11... | collective-permute-start | bytes 1474568 | tf_op jit(solution)/shard_map/ppermute | solution.py:277
  238.5 12.2 %copy-start.22 = (s32[4]{0:T(128)S(1)}, s32[4]{0:T(128)}, u32[]{:S(2)}) copy-start(s32[4]{0:T(128)} %copy-done.21) | copy-start | bytes 52
  238.5 27.1 %collective-permute-start.30 = (bf16[240,1024]{1,0:T(8,128)(2,1)}, bf16[240,1024]{1,0:T(8,128)(2,1)}, u32[]{:S(2)}, u32[]{:S(2)}) collective-permute-start(bf16[240,1024]{1,0:T(8,128)(2,1)} %collective-permute-done.28.refs_2_), channel_id=1, source_target_pairs={{0,4},{1,3},{4,8},{5,1},{8,12},{9,5},{12,14},{13,9},{14,10},{15,13... | collective-permute-start | bytes 1474568 | tf_op jit(solution)/shard_map/ppermute | solution.py:276
  238.8 1.0 copy-start.3
  248.8 21.8 %collective-permute-start.29 = (bf16[240,1024]{1,0:T(8,128)(2,1)}, bf16[240,1024]{1,0:T(8,128)(2,1)}, u32[]{:S(2)}, u32[]{:S(2)}) collective-permute-start(bf16[240,1024]{1,0:T(8,128)(2,1)} %collective-permute-done.28.refs_2_), channel_id=1, source_target_pairs={{0,1},{1,0},{2,3},{3,2},{4,5},{5,4},{6,7},{7,6},{8,9},{9,8},{10,11... | collective-permute-start | bytes 1474568 | tf_op jit(solution)/shard_map/ppermute | solution.py:277
  263.5 7.0 %copy-start.20 = (s32[4]{0:T(128)S(1)}, s32[4]{0:T(128)}, u32[]{:S(2)}) copy-start(s32[4]{0:T(128)} %copy-done.19) | copy-start | bytes 52
  265.5 22.3 %collective-permute-start.31 = (bf16[240,1024]{1,0:T(8,128)(2,1)}, bf16[240,1024]{1,0:T(8,128)(2,1)}, u32[]{:S(2)}, u32[]{:S(2)}) collective-permute-start(bf16[240,1024]{1,0:T(8,128)(2,1)} %collective-permute-done.30.refs_2_), channel_id=1, source_target_pairs={{0,1},{1,0},{2,3},{3,2},{4,5},{5,4},{6,7},{7,6},{8,9},{9,8},{10,11... | collective-permute-start | bytes 1474568 | tf_op jit(solution)/shard_map/ppermute | solution.py:277
  269.3 18.0 %collective-permute-start.32 = (bf16[240,512]{1,0:T(8,128)(2,1)}, bf16[240,512]{1,0:T(8,128)(2,1)}, u32[]{:S(2)}, u32[]{:S(2)}) collective-permute-start(bf16[240,512]{1,0:T(8,128)(2,1)} %slice.254), channel_id=1, source_target_pairs={{0,4},{1,3},{4,8},{5,1},{8,12},{9,5},{12,14},{13,9},{14,10},{15,13... | collective-permute-start | bytes 737288 | tf_op jit(solution)/shard_map/ppermute | solution.py:276
  282.6 0.8 copy-start.7
  283.4 4.5 %copy-start.18 = (s32[4]{0:T(128)S(1)}, s32[4]{0:T(128)}, u32[]{:S(2)}) copy-start(s32[4]{0:T(128)} %copy-done.17) | copy-start | bytes 52
  287.3 17.3 %collective-permute-start.33 = (bf16[240,512]{1,0:T(8,128)(2,1)}, bf16[240,512]{1,0:T(8,128)(2,1)}, u32[]{:S(2)}, u32[]{:S(2)}) collective-permute-start(bf16[240,512]{1,0:T(8,128)(2,1)} %collective-permute-done.32.refs_2_), channel_id=1, source_target_pairs={{0,1},{1,0},{2,3},{3,2},{4,5},{5,4},{6,7},{7,6},{8,9},{9,8},{10,11... | collective-permute-start | bytes 737288 | tf_op jit(solution)/shard_map/ppermute | solution.py:277
  299.9 0.8 copy-start.8
  300.7 3.9 copy-start.16
  366.9 24.1 %copy-start.28 = (pred[240,240]{1,0:T(8,128)(4,1)S(1)}, pred[240,240]{1,0:T(8,128)(4,1)}, u32[]{:S(2)}) copy-start(pred[240,240]{1,0:T(8,128)(4,1)} %iota_compare_fusion.2) | copy-start | bytes 172804
  368.9 23.2 %collective-permute-start.34 = (f32[120,240]{1,0:T(8,128)}, f32[120,240]{1,0:T(8,128)}, u32[]{:S(2)}, u32[]{:S(2)}) collective-permute-start(f32[120,240]{1,0:T(8,128)} %slice_select_fusion), channel_id=1, source_target_pairs={{0,1},{1,0},{2,3},{3,2},{4,5},{5,4},{6,7},{7,6},{8,9},{9,8},{10,11... | collective-permute-start | bytes 345608 | tf_op jit(solution)/shard_map/ppermute | solution.py:291
  391.0 20.2 %copy-start.25 = (f32[240,1024]{1,0:T(8,128)S(1)}, f32[240,1024]{1,0:T(8,128)}, u32[]{:S(2)}) copy-start(f32[240,1024]{1,0:T(8,128)} %get-tuple-element.76) | copy-start | bytes 2949124
  393.2 4.4 %collective-permute-start.35 = (f32[120,240]{1,0:T(8,128)S(1)}, f32[120,240]{1,0:T(8,128)S(1)}, u32[]{:S(2)}, u32[]{:S(2)}) collective-permute-start(f32[120,240]{1,0:T(8,128)S(1)} %select_add_fusion), channel_id=1, source_target_pairs={{0,2},{1,3},{2,0},{3,1},{4,6},{5,7},{6,4},{7,5},{8,10},{9,11},{10,... | collective-permute-start | bytes 345608 | tf_op jit(solution)/shard_map/ppermute | solution.py:295
  397.7 3.8 collective-permute-start.36
  401.5 6.0 %collective-permute-start.37 = (f32[120,240]{1,0:T(8,128)S(1)}, f32[120,240]{1,0:T(8,128)S(1)}, u32[]{:S(2)}, u32[]{:S(2)}) collective-permute-start(f32[120,240]{1,0:T(8,128)S(1)} %add.335), channel_id=1, source_target_pairs={{0,8},{1,9},{2,10},{3,11},{4,12},{5,13},{6,14},{7,15},{8,0},{9,1},... | collective-permute-start | bytes 345608 | tf_op jit(solution)/shard_map/ppermute | solution.py:295
  403.8 8.8 %copy-start.23 = (f32[240,224]{0,1:T(8,128)}, f32[240,224]{0,1:T(8,128)S(1)}, u32[]{:S(2)}) copy-start(f32[240,224]{0,1:T(8,128)S(1)} %fusion.7) | copy-start | bytes 645124
  407.5 5.1 %collective-permute-start.38 = (f32[120,240]{1,0:T(8,128)S(1)}, f32[120,240]{1,0:T(8,128)S(1)}, u32[]{:S(2)}, u32[]{:S(2)}) collective-permute-start(f32[120,240]{1,0:T(8,128)S(1)} %add.336), channel_id=1, source_target_pairs={{0,1},{1,0},{2,3},{3,2},{4,5},{5,4},{6,7},{7,6},{8,9},{9,8},{10,11... | collective-permute-start | bytes 345608 | tf_op jit(solution)/shard_map/ppermute | solution.py:297
  (7 other events, 5.0 us)

commit v2 on v1

--- a/solution.py
+++ b/solution.py
@@ -100,72 +100,178 @@
         return {name: row[at : at + size] for name, (at, size) in self.width.items()}
 
 
-def columns_kernel(kept, ids_ref, left_ref, weight_ref, keep_ref, *give):
-    step = pl.program_id(0)
+def columns_kernel(kept, cuts, ids_ref, left_ref, weight_ref, keep_ref, *rest):
+    step, cut = pl.program_id(0), pl.program_id(1)
     part = jnp.dot(left_ref[...], weight_ref[...], preferred_element_type=jnp.float32)
-    if not give:
-        keep_ref[...] = part
-        return
-
-    @pl.when(step < kept)
-    def _():
-        keep_ref[...] = part
-
-    @pl.when(step >= kept)
-    def _():
-        give[0][...] = part.astype(jnp.bfloat16)
-
-
-def column_sums(left, weight, halves, half, split):
+    if cuts > 1:
+        total_ref = rest[-1]
+
+        @pl.when(cut == 0)
+        def _():
+            total_ref[...] = part
+
+        @pl.when((cut > 0) & (cut < cuts - 1))
+        def _():
+            total_ref[...] += part
+
+    def finish():
+        total = total_ref[...] + part if cuts > 1 else part
+
+        @pl.when(step < kept)
+        def _():
+            keep_ref[...] = total
+
+        @pl.when(step >= kept)
+        def _():
+            rest[0][...] = total.astype(jnp.bfloat16)
+
+    def finish_all():
+        keep_ref[...] = total_ref[...] + part if cuts > 1 else part
+
+    pl.when(cut == cuts - 1)(finish if kept is not None else finish_all)
+
+
+def column_sums(left, weight, ids, half, split, cuts):
     rows, wide = left.shape[1], left.shape[0]
-    block = min(256, half)
-    per = half // block
-    ids = (halves[:, None] * per + jnp.arange(per, dtype=jnp.int32)[None, :]).reshape(-1)
-    steps = ids.shape[0]
+    steps, tall = ids.shape[0], rows // cuts
     kept = steps // 2 if split else steps
-    out_shape = [jax.ShapeDtypeStruct((wide, kept * block), jnp.float32)]
-    out_specs = [pl.BlockSpec((wide, block), lambda j, ids: (0, jnp.minimum(j, kept - 1)))]
+    out_shape = [jax.ShapeDtypeStruct((wide, kept * half), jnp.float32)]
+    out_specs = [pl.BlockSpec((wide, half), lambda j, c, ids: (0, jnp.minimum(j, kept - 1)))]
     if split:
-        out_shape.append(jax.ShapeDtypeStruct((wide, kept * block), jnp.bfloat16))
-        out_specs.append(pl.BlockSpec((wide, block), lambda j, ids: (0, jnp.maximum(j - kept, 0))))
+        out_shape.append(jax.ShapeDtypeStruct((wide, kept * half), jnp.bfloat16))
+        out_specs.append(pl.BlockSpec((wide, half), lambda j, c, ids: (0, jnp.maximum(j - kept, 0))))
     return pl.pallas_call(
-        functools.partial(columns_kernel, kept),
+        functools.partial(columns_kernel, kept if split else None, cuts),
         out_shape=out_shape,
         grid_spec=pltpu.PrefetchScalarGridSpec(
             num_scalar_prefetch=1,
-            grid=(steps,),
+            grid=(steps, cuts),
             in_specs=[
-                pl.BlockSpec((wide, rows), lambda j, ids: (0, 0)),
-                pl.BlockSpec((rows, block), lambda j, ids: (0, ids[j])),
+                pl.BlockSpec((wide, tall), lambda j, c, ids: (0, c)),
+                pl.BlockSpec((tall, half), lambda j, c, ids: (c, ids[j])),
             ],
             out_specs=out_specs,
+            scratch_shapes=[pltpu.VMEM((wide, half), jnp.float32)] if cuts > 1 else [],
         ),
         compiler_params=pltpu.CompilerParams(
-            dimension_semantics=("arbitrary",), vmem_limit_bytes=32 * MIB
+            dimension_semantics=("arbitrary", "arbitrary"), vmem_limit_bytes=32 * MIB
         ),
         cost_estimate=pl.CostEstimate(
-            flops=2 * wide * rows * steps * block,
-            bytes_accessed=2 * rows * steps * block + 2 * rows * wide,
+            flops=2 * wide * rows * steps * half,
+            bytes_accessed=2 * rows * steps * half + 2 * rows * wide,
             transcendentals=0,
         ),
     )(ids, left, weight)
 
 
-def rows_kernel(pieces, halves, chained, turned, with_gram, *refs):
+def invert_kernel(counts, order_ref, *refs):
+    grams, out_ref = refs[:len(counts)], refs[len(counts)]
+    all_ref, work_ref = refs[len(counts) + 1 :]
+    at = 0
+    for ref, count in zip(grams, counts):
+        all_ref[at : at + count] = ref[...]
+        at += count
+    size = work_ref.shape[0]
+    total = all_ref[order_ref[0]]
+    for chip in range(1, at):
+        total = total + all_ref[order_ref[chip]]
+    work_ref[...] = jnp.zeros_like(work_ref)
+    work_ref[:, :size] = total
+    lanes = lax.broadcasted_iota(jnp.int32, (8, 128), 1)
+    panels = size // 8
+    for first in range(0, panels, 8):
+        side = first // 16
+        tall = size - 8 * first
+
+        def panel(p, _, first=first, side=side, tall=tall):
+            body = work_ref[8 * first :, :]
+            low, high = body[:, :128], body[:, 128:]
+            sides = [low, high]
+            block = [work_ref[pl.ds(8 * p, 8), :128], work_ref[pl.ds(8 * p, 8), 128:]]
+            below = lax.broadcasted_iota(jnp.int32, (tall, 128), 0) - 8 * (p - first)
+            inside = lax.broadcasted_iota(jnp.int32, (8, 128), 0)
+            pivots = jnp.zeros((8, 128), jnp.float32)
+            for s in range(8):
+                lane = 8 * p + s - 128 * side
+                here = lanes == lane
+                rows = [jnp.broadcast_to(b[s : s + 1], (8, 128)) for b in block]
+                at = jnp.full((8, 128), lane, jnp.int32)
+                pivot = jnp.take_along_axis(rows[side], at, axis=1)
+                inverse = 1.0 / pivot
+                pivots = jnp.where(inside == s, pivot, pivots)
+                rows[side] = jnp.where(here, 1.0, rows[side])
+
+                def reduce(parts, beyond):
+                    count = parts[0].shape[0] // 8
+                    spread = lambda x: jnp.tile(x, (count, 1)) if count > 1 else x
+                    column = jnp.take_along_axis(parts[side], spread(at), axis=1)
+                    factor = jnp.where(beyond, column * spread(inverse), 0.0)
+                    parts = list(parts)
+                    parts[side] = jnp.where(spread(here) & beyond, 0.0, parts[side])
+                    return [part - factor * spread(row) for part, row in zip(parts, rows)]
+
+                if s < 7:
+                    block = reduce(block, inside > s)
+                else:
+                    block[side] = block[side]
+                sides = reduce(sides, below > s)
+            work_ref[8 * first :, :128] = sides[0]
+            work_ref[8 * first :, 128:] = sides[1]
+            scale = lax.rsqrt(pivots)
+            final = [work_ref[pl.ds(8 * p, 8), :128], work_ref[pl.ds(8 * p, 8), 128:]]
+            both = jnp.concatenate([final[0] * scale, final[1] * scale], 1)
+            columns = lax.broadcasted_iota(jnp.int32, (8, 256), 1)
+            rows_at = lax.broadcasted_iota(jnp.int32, (8, 256), 0) + 8 * p
+            both = jnp.where(columns == rows_at, jnp.concatenate([scale, scale], 1), both)
+            both = jnp.where(columns > rows_at, 0.0, both)
+            out_ref[pl.ds(8 * p, 8), :] = both[:, :size]
+            return 0
+
+        lax.fori_loop(first, min(first + 8, panels), panel, 0)
+
+def invert(order, grams):
+    size = grams[0].shape[-1]
+    counts = [g.shape[0] for g in grams]
+    return pl.pallas_call(
+        functools.partial(invert_kernel, counts),
+        out_shape=jax.ShapeDtypeStruct((size, size), jnp.float32),
+        grid_spec=pltpu.PrefetchScalarGridSpec(
+            num_scalar_prefetch=1, grid=(),
+            in_specs=[pl.BlockSpec(memory_space=pltpu.VMEM)] * len(grams),
+            out_specs=pl.BlockSpec(memory_space=pltpu.VMEM),
+            scratch_shapes=[pltpu.VMEM((sum(counts), size, size), jnp.float32), pltpu.VMEM((size, 256), jnp.float32)],
+        ),
+        compiler_params=pltpu.CompilerParams(vmem_limit_bytes=32 * MIB),
+    )(order, *grams)
+
+
+def rows_kernel(pieces, halves, chained, last, turned, with_gram, *refs):
     refs = list(refs[1:])
     weight_ref = refs.pop(0)
     piece_refs = [refs.pop(0) for _ in range(pieces)]
     before_ref = refs.pop(0) if chained else None
     out_ref = refs.pop(0)
     gram_ref = refs.pop(0) if with_gram else None
-    total_ref = refs.pop(0) if turned else out_ref
+    narrow = out_ref.dtype != jnp.float32
+    total_ref = refs.pop(0) if narrow else out_ref
     block, step = pl.program_id(0), pl.program_id(1)
     steps = pieces * halves
-    piece = piece_refs[0][...]
-    if pieces == 2:
-        piece = jnp.where(step < halves, piece, piece_refs[1][...])
     onto = (((1,), (1,)), ((), ()))
-    part = lax.dot_general(weight_ref[...], piece, onto, preferred_element_type=jnp.float32)
+
+    def chosen():
+        piece = piece_refs[0][...]
+        return piece if pieces == 1 else jnp.where(step < halves, piece, piece_refs[1][...])
+
+    if turned:
+        part = lax.dot_general(chosen(), weight_ref[...], onto, preferred_element_type=jnp.float32)
+    else:
+        upright_ref = refs.pop(0)
+
+        @pl.when(block == 0)
+        def _():
+            upright_ref[step] = chosen().astype(jnp.float32).T.astype(jnp.bfloat16)
+
+        part = jnp.dot(weight_ref[...], upright_ref[step], preferred_element_type=jnp.float32)
 
     @pl.when(step == 0)
     def _():
@@ -175,11 +281,11 @@
     def _():
         total_ref[...] += part
 
-    if turned:
+    if narrow:
 
         @pl.when(step == steps - 1)
         def _():
-            out_ref[...] = total_ref[...].T.astype(jnp.bfloat16)
+            out_ref[...] = total_ref[...].astype(jnp.bfloat16)
 
     if with_gram:
         slots = gram_ref.shape[0]
@@ -187,6 +293,7 @@
 
         @pl.when(block == 0)
         def _():
+            piece = chosen()
             square = lax.dot_general(piece, piece, onto, preferred_element_type=jnp.float32)
             slot = step // run
 
@@ -199,11 +306,14 @@
                 gram_ref[slot] += square
 
 
-def row_products(weight, pieces, ids, half, before, turned, with_gram):
+def row_products(weight, pieces, ids, half, before, last, turned, with_gram):
     rows, wide = weight.shape[0], pieces[0].shape[0]
     halves = pieces[0].shape[1] // half
     steps = len(pieces) * halves
     tall = rows // 2 if rows % 256 == 0 else rows
+    shape, tile = ((wide, rows), (wide, tall)) if turned else ((rows, wide), (tall, wide))
+    place = (lambda i, j, ids: (0, i)) if turned else (lambda i, j, ids: (i, 0))
+    narrow = turned and last
 
     def piece_spec(at):
         low = at * halves
@@ -213,29 +323,30 @@
     in_specs += [piece_spec(at) for at in range(len(pieces))]
     operands = [weight, *pieces]
     if before is not None:
-        in_specs.append(pl.BlockSpec((tall, wide), lambda i, j, ids: (i, 0)))
+        in_specs.append(pl.BlockSpec(tile, place))
         operands.append(before)
-    if turned:
-        out_shape = [jax.ShapeDtypeStruct((wide, rows), jnp.bfloat16)]
-        out_specs = [pl.BlockSpec((wide, tall), lambda i, j, ids: (0, i))]
-    else:
-        out_shape = [jax.ShapeDtypeStruct((rows, wide), jnp.float32)]
-        out_specs = [pl.BlockSpec((tall, wide), lambda i, j, ids: (i, 0))]
+    out_shape = [jax.ShapeDtypeStruct(shape, jnp.bfloat16 if narrow else jnp.float32)]
+    out_specs = [pl.BlockSpec(tile, place)]
     if with_gram:
         slots = max(1, steps // 2)
         out_shape.append(jax.ShapeDtypeStruct((slots, wide, wide), jnp.float32))
         out_specs.append(pl.BlockSpec((slots, wide, wide), lambda i, j, ids: (0, 0, 0)))
+    scratch = [pltpu.VMEM(tile, jnp.float32)] if narrow else []
+    if not turned:
+        scratch.append(pltpu.VMEM((steps, half, wide), jnp.bfloat16))
     return pl.pallas_call(
-        functools.partial(rows_kernel, len(pieces), halves, before is not None, turned, with_gram),
+        functools.partial(
+            rows_kernel, len(pieces), halves, before is not None, last, turned, with_gram
+        ),
         out_shape=out_shape,
         grid_spec=pltpu.PrefetchScalarGridSpec(
             num_scalar_prefetch=1,
             grid=(rows // tall, steps),
             in_specs=in_specs,
             out_specs=out_specs,
-            scratch_shapes=[pltpu.VMEM((tall, wide), jnp.float32)] if turned else [],
-        ),
-        input_output_aliases={len(operands): 0} if before is not None and not turned else {},
+            scratch_shapes=scratch,
+        ),
+        input_output_aliases={len(operands): 0} if before is not None and not narrow else {},
         compiler_params=pltpu.CompilerParams(
             dimension_semantics=("arbitrary", "arbitrary"), vmem_limit_bytes=40 * MIB
         ),
@@ -247,10 +358,10 @@
     )(ids, *operands)
 
 
-def ring_sum(ring, ids, left, weight, half):
+def ring_sum(ring, ids, left, weight, half, cuts):
     got = None
     for k in range(ring.far, 0, -1):
-        keep, give = column_sums(left, weight, ids["sum", k], half, True)
+        keep, give = column_sums(left, weight, ids["sum", k], half, True, cuts)
         total = keep + lax.ppermute(give, "row", ring.pair).astype(jnp.float32)
         if got is not None:
             got = got.astype(jnp.float32)
@@ -259,8 +370,9 @@
                 total = jnp.concatenate([total[:, :size] + got, total[:, size:]], 1)
             else:
                 total = total + got
-        got = lax.ppermute(total.astype(jnp.bfloat16), "row", ring.ahead)
-    (keep,) = column_sums(left, weight, ids["sum", 0], half, False)
+        total, left = lax.optimization_barrier((total.astype(jnp.bfloat16), left))
+        got = lax.ppermute(total, "row", ring.ahead)
+    (keep,) = column_sums(left, weight, ids["sum", 0], half, False, cuts)
     mine = keep + got.astype(jnp.float32)
     other = lax.ppermute(mine, "row", ring.pair)
     return mine + jnp.concatenate([other[:, half:], other[:, :half]], 1)
@@ -274,10 +386,11 @@
             pieces = [chunk]
         else:
             moving = lax.ppermute(moving if k < ring.far else moving[:, :half], "row", ring.ahead)
+            moving, before = lax.optimization_barrier((moving, before))
             pieces = [moving, lax.ppermute(moving, "row", ring.pair)]
         last = k == ring.far
         before, *gram = row_products(
-            weight, pieces, ids["use", k], half, before, turned and last, with_gram
+            weight, pieces, ids["use", k], half, before, last, turned, with_gram
         )
         grams += gram
     return before, grams
@@ -304,9 +417,9 @@
     half = features // (2 * ring.chips)
     ids = ring.row()
     picker = selector(rank_mask, RANK)
-    sketch = ring_sum(ring, ids, test_matrix.T, weight, half).astype(jnp.bfloat16)
+    sketch = ring_sum(ring, ids, test_matrix.T, weight, half, 1).astype(jnp.bfloat16)
     mixed, _ = ring_apply(ring, ids, sketch, weight, half, True, False)
-    powered = ring_sum(ring, ids, mixed, weight, half)
+    powered = ring_sum(ring, ids, mixed, weight, half, 2)
     image, grams = ring_apply(
         ring, ids, powered.astype(jnp.bfloat16), weight, half, False, True
     )
@@ -315,20 +428,8 @@
         image_b, image_b, (((0,), (0,)), ((), ())), preferred_element_type=jnp.float32
     )
     square = group_sum(square, ring)
-    stack = jnp.concatenate(grams, 0)
-    gram_matrix = sum(
-        lax.dynamic_index_in_dim(stack, ids["arrival"][chip], 0, keepdims=False)
-        for chip in range(ring.chips)
-    )
-    cholesky_factor = jnp.linalg.cholesky(gram_matrix)
-    inverse = lax.linalg.triangular_solve(
-        cholesky_factor,
-        jnp.eye(gram_matrix.shape[0], dtype=jnp.float32),
-        left_side=False,
-        lower=True,
-        transpose_a=True,
-    )
-    change = jnp.dot(inverse, picker, precision=highest)
+    inverse = invert(ids["arrival"], grams)
+    change = lax.dot_general(inverse, picker, (((0,), (0,)), ((), ())), precision=highest)
     own = powered[:, :half]
     left_factor = lax.dot_general(
         own, change, (((0,), (0,)), ((), ())), precision=highest

time: 430 us -> 297 us (0.69); the launches traced: 422 us -> 295 us
  other arithmetic: 74.9 us -> 3.65 us
  local copies, waits for them, and re-layouts: 35.5 us -> 6.07 us
  between operations: 20.2 us -> 3.11 us
  Pallas kernels: 180 us -> 196 us
  waiting for transfers between devices: 61.5 us -> 48 us
  matrix products: 15.1 us -> 9.16 us
  starting transfers between devices: 34.7 us -> 28.9 us
    another operation x18 -> x5, other arithmetic: 61 us -> 0.55 us  [the longest x7 37.4 us: ring_body(): cholesky_factor = jnp.linalg.cholesky(gram_matrix)]
    ppermute x8, waiting for transfers between devices: 21.3 us -> 1.71 us  [ring_apply(): lax.ppermute(moving if k < ring.far else moving[:, :half], 'row', ring.ah...]
    pallas_call x10 -> x11, Pallas kernels: 83 us -> 99.3 us  [the longest x10 77 us: column_sums(): pl.pallas_call(functools.partial(columns_kernel, kept if split else None,...]
    ppermute x8, waiting for transfers between devices: 26.4 us -> 12.3 us  [ring_sum(): got = lax.ppermute(total, 'row', ring.ahead)]
    unnamed x68 -> x62, local copies, waits for them, and re-layouts: 17.3 us -> 3.78 us
    pallas_call x5 -> x0, local copies, waits for them, and re-layouts: 9.56 us -> none  [row_products(): pl.pallas_call(functools.partial(rows_kernel, len(pieces), halves, before...]
    ppermute x8, waiting for transfers between devices: 1.06 us -> 9.77 us  [ring_sum(): total = keep + lax.ppermute(give, 'row', ring.pair).astype(jnp.float32)]
    ppermute x8, waiting for transfers between devices: 0.02 us -> 8.33 us  [ring_apply(): pieces = [moving, lax.ppermute(moving, 'row', ring.pair)]]
  transfers between devices with their start and end apart: 39 -> 39, of which waited for: 15 -> 25; matrix products, arithmetic and copies ran while one was open for 12% -> 1% of each run, Pallas kernels for 33% -> 52%
where the time goes in v2:
time: 297 us; the launch traced here: 295 us
  Pallas kernels  196 us (66%)
  waiting for transfers between devices  48 us (16%)
  starting transfers between devices  28.9 us (10%)
  matrix products  9.16 us (3%)
  local copies, waits for them, and re-layouts  6.07 us (2%)
  other arithmetic  3.65 us (1%)
  between operations  3.11 us (1%)
    pallas_call x10, Pallas kernels, row_products(): pl.pallas_call(functools.partial(rows_kernel, len(pieces), halves, before...  96.9 us
    pallas_call x10, Pallas kernels, column_sums(): pl.pallas_call(functools.partial(columns_kernel, kept if split else None,...  77 us
    pallas_call x1, Pallas kernels, invert(): pl.pallas_call(functools.partial(invert_kernel, counts), out_shape=jax.Sh...  22.3 us
    ppermute x8, waiting for transfers between devices, ring_sum(): got = lax.ppermute(total, 'row', ring.ahead)  12.3 us
    ppermute x3, waiting for transfers between devices, group_sum(): part = part + lax.ppermute(part, 'row', swap)  10.5 us
    ppermute x8, waiting for transfers between devices, ring_sum(): total = keep + lax.ppermute(give, 'row', ring.pair).astype(jnp.float32)  9.77 us
    ppermute x8, starting transfers between devices, ring_sum(): total = keep + lax.ppermute(give, 'row', ring.pair).astype(jnp.float32)  8.39 us
    ppermute x8, waiting for transfers between devices, ring_apply(): pieces = [moving, lax.ppermute(moving, 'row', ring.pair)]  8.33 us
  transfers between devices with their start and end apart: 39, of which 25 were waited for; matrix products, arithmetic and copies ran while one was open for 1% of the time, Pallas kernels for 52%

profile of v2, /device:TPU:1, one launch (start us, length us, event | category | flops | bytes accessed | tf_op | source)
XLA Modules:
  0.0 295.1 jit_solution(78377583127210669)
XLA Ops:
  1.4 1.4 copy-done
  2.8 4.6 %shard_map.67 = (f32[240,512]{1,0:T(8,128)S(1)}, bf16[240,512]{1,0:T(8,128)(2,1)S(1)}) custom-call(s32[2]{0:T(128)S(1)} %get-tuple-element.135.ids_ref, bf16[240,3328]{1,0:T(8,128)(2,1)S(1)} %bitcast.34, bf16[3328,8192]{1,0:T(8,128)(2,1)} %refs_1_.19), custom_call_target="tpu_custom_call" | custom-call | flops 1635778560 | bytes 8413184 | tf_op jit(solution)/shard_map/pallas_call | solution.py:143
  7.7 1.4 collective-permute-done
  9.1 7.9 %shard_map.68 = (f32[240,1024]{1,0:T(8,128)S(1)}, bf16[240,1024]{1,0:T(8,128)(2,1)S(1)}) custom-call(s32[4]{0:T(128)S(1)} %get-tuple-element.130.ids_ref, bf16[240,3328]{1,0:T(8,128)(2,1)S(1)} %bitcast.35, bf16[3328,8192]{1,0:T(8,128)(2,1)} %refs_1_.19), custom_call_target="tpu_custom_call" | custom-call | flops 3271557120 | bytes 15228928 | tf_op jit(solution)/shard_map/pallas_call | solution.py:143
  17.2 2.6 collective-permute-start.2
  20.1 3.7 %collective-permute-done.2 = bf16[240,512]{1,0:T(8,128)(2,1)S(1)} collective-permute-done((bf16[240,512]{1,0:T(8,128)(2,1)S(1)}, bf16[240,512]{1,0:T(8,128)(2,1)S(1)}, u32[]{:S(2)}, u32[]{:S(2)}) %collective-permute-start.2) | collective-permute-done | bytes 245792 | tf_op jit(solution)/shard_map/ppermute | solution.py:374
  23.9 1.5 collective-permute-start.4
  25.4 7.9 %shard_map.69 = (f32[240,1024]{1,0:T(8,128)S(1)}, bf16[240,1024]{1,0:T(8,128)(2,1)S(1)}) custom-call(s32[4]{0:T(128)S(1)} %get-tuple-element.131.ids_ref, bf16[240,3328]{1,0:T(8,128)(2,1)S(1)} %bitcast.36, bf16[3328,8192]{1,0:T(8,128)(2,1)} %refs_1_.19), custom_call_target="tpu_custom_call" | custom-call | flops 3271557120 | bytes 15228928 | tf_op jit(solution)/shard_map/pallas_call | solution.py:143
  33.3 1.4 collective-permute-start.3
  34.7 1.5 collective-permute-done.3
  36.8 7.9 %shard_map.70 = (f32[240,1024]{1,0:T(8,128)S(1)}, bf16[240,1024]{1,0:T(8,128)(2,1)S(1)}) custom-call(s32[4]{0:T(128)S(1)} %get-tuple-element.132.ids_ref, bf16[240,3328]{1,0:T(8,128)(2,1)S(1)} %bitcast.37, bf16[3328,8192]{1,0:T(8,128)(2,1)} %refs_1_.19), custom_call_target="tpu_custom_call" | custom-call | flops 3271557120 | bytes 15228928 | tf_op jit(solution)/shard_map/pallas_call | solution.py:143
  44.8 1.7 collective-permute-start.5
  46.4 1.5 collective-permute-done.5
  48.4 4.6 %shard_map.71 = f32[240,1024]{1,0:T(8,128)S(1)} custom-call(s32[2]{0:T(128)S(1)} %get-tuple-element.136.ids_ref, bf16[240,3328]{1,0:T(8,128)(2,1)S(1)} %bitcast.38, bf16[3328,8192]{1,0:T(8,128)(2,1)} %refs_1_.19), custom_call_target="tpu_custom_call" | custom-call | flops 1635778560 | bytes 8413184 | tf_op jit(solution)/shard_map/pallas_call | solution.py:143
  53.0 3.2 %collective-permute-done.7 = bf16[240,1024]{1,0:T(8,128)(2,1)S(1)} collective-permute-done((bf16[240,1024]{1,0:T(8,128)(2,1)S(1)}, bf16[240,1024]{1,0:T(8,128)(2,1)S(1)}, u32[]{:S(2)}, u32[]{:S(2)}) %collective-permute-start.7) | collective-permute-done | bytes 491552 | tf_op jit(solution)/shard_map/ppermute | solution.py:374
  56.4 1.3 collective-permute-start.8
  57.7 2.2 collective-permute-done.8
  60.3 6.3 %shard_map.72.refs_4_ = f32[240,3328]{1,0:T(8,128)S(1)} custom-call(s32[2]{0:T(128)S(1)} %get-tuple-element.134.refs_0_, bf16[3328,8192]{1,0:T(8,128)(2,1)} %refs_1_.19, bf16[240,1024]{1,0:T(8,128)(2,1)S(1)} %fusion.3.refs_2_), custom_call_target="tpu_custom_call" | custom-call | flops 1635778560 | bytes 13205504 | tf_op jit(solution)/shard_map/pallas_call | solution.py:337
  66.6 1.5 collective-permute-done.9.refs_2_
  68.1 1.2 collective-permute-start.11
  69.5 1.3 collective-permute-done.11.refs_3_
  70.8 11.3 %shard_map.73.refs_4_ = f32[240,3328]{1,0:T(8,128)S(1)} custom-call(s32[4]{0:T(128)S(1)} %get-tuple-element.129.refs_0_, bf16[3328,8192]{1,0:T(8,128)(2,1)} %refs_1_.19, bf16[240,1024]{1,0:T(8,128)(2,1)S(1)} %collective-permute-done.9.refs_2_, bf16[240,1024]{1,0:T(8,128)(2,1)S(1)} %collective-permute-done.11.refs_3_, ...), custom_call_target="tpu_custom_call", output_to_operand_aliasing={{}: (4, {})} | custom-call | flops 3271557120 | bytes 20021248 | tf_op jit(solution)/shard_map/pallas_call | solution.py:337
  82.8 1.3 collective-permute-done.13.refs_3_
  84.1 11.3 %shard_map.74.refs_4_ = f32[240,3328]{1,0:T(8,128)S(1)} custom-call(s32[4]{0:T(128)S(1)} %get-tuple-element.128.refs_0_, bf16[3328,8192]{1,0:T(8,128)(2,1)} %refs_1_.19, bf16[240,1024]{1,0:T(8,128)(2,1)S(1)} %collective-permute-done.10.refs_2_, bf16[240,1024]{1,0:T(8,128)(2,1)S(1)} %collective-permute-done.13.refs_3_, ...), custom_call_target="tpu_custom_call", output_to_operand_aliasing={{}: (4, {})} | custom-call | flops 3271557120 | bytes 20021248 | tf_op jit(solution)/shard_map/pallas_call | solution.py:337
  96.2 1.1 collective-permute-done.15.refs_3_
  97.3 11.3 %shard_map.75.refs_4_ = f32[240,3328]{1,0:T(8,128)S(1)} custom-call(s32[4]{0:T(128)S(1)} %get-tuple-element.127.refs_0_, bf16[3328,8192]{1,0:T(8,128)(2,1)} %refs_1_.19, bf16[240,1024]{1,0:T(8,128)(2,1)S(1)} %collective-permute-done.12.refs_2_, bf16[240,1024]{1,0:T(8,128)(2,1)S(1)} %collective-permute-done.15.refs_3_, ...), custom_call_target="tpu_custom_call", output_to_operand_aliasing={{}: (4, {})} | custom-call | flops 3271557120 | bytes 20021248 | tf_op jit(solution)/shard_map/pallas_call | solution.py:337
  109.1 1.1 collective-permute-done.16.refs_3_
  110.2 6.5 %shard_map.76.left_ref = bf16[240,3328]{1,0:T(8,128)(2,1)S(1)} custom-call(s32[2]{0:T(128)S(1)} %get-tuple-element.133.refs_0_, bf16[3328,8192]{1,0:T(8,128)(2,1)} %refs_1_.19, bf16[240,512]{1,0:T(8,128)(2,1)S(1)} %collective-permute-done.14.refs_2_, bf16[240,512]{1,0:T(8,128)(2,1)S(1)} %collective-permute-done.16.refs_3_, f32[240,3328]{1,0:T(8,128)S(1)} %shard_map.75.refs_4_), custom_call_target="tpu_custom_call" | custom-call | flops 1635778560 | bytes 13205504 | tf_op jit(solution)/shard_map/pallas_call | solution.py:337
  116.8 5.9 %shard_map.77 = (f32[240,512]{1,0:T(8,128)S(1)}, bf16[240,512]{1,0:T(8,128)(2,1)S(1)}) custom-call(s32[2]{0:T(128)S(1)} %copy-done.19, bf16[240,3328]{1,0:T(8,128)(2,1)S(1)} %shard_map.76.left_ref, bf16[3328,8192]{1,0:T(8,128)(2,1)} %refs_1_.19), custom_call_target="tpu_custom_call" | custom-call | flops 1635778560 | bytes 8413184 | tf_op jit(solution)/shard_map/pallas_call | solution.py:143
  123.1 1.1 collective-permute-done.17
  124.3 10.7 %shard_map.78 = (f32[240,1024]{1,0:T(8,128)S(1)}, bf16[240,1024]{1,0:T(8,128)(2,1)S(1)}) custom-call(s32[4]{0:T(128)S(1)} %copy-done.17, bf16[240,3328]{1,0:T(8,128)(2,1)S(1)} %shard_map.76.left_ref, bf16[3328,8192]{1,0:T(8,128)(2,1)} %refs_1_.19), custom_call_target="tpu_custom_call" | custom-call | flops 3271557120 | bytes 15228928 | tf_op jit(solution)/shard_map/pallas_call | solution.py:143
  135.7 1.3 collective-permute-done.18
  137.2 3.6 %collective-permute-done.19 = bf16[240,512]{1,0:T(8,128)(2,1)S(1)} collective-permute-done((bf16[240,512]{1,0:T(8,128)(2,1)S(1)}, bf16[240,512]{1,0:T(8,128)(2,1)S(1)}, u32[]{:S(2)}, u32[]{:S(2)}) %collective-permute-start.19) | collective-permute-done | bytes 245792 | tf_op jit(solution)/shard_map/ppermute | solution.py:374
  141.2 10.7 %shard_map.79 = (f32[240,1024]{1,0:T(8,128)S(1)}, bf16[240,1024]{1,0:T(8,128)(2,1)S(1)}) custom-call(s32[4]{0:T(128)S(1)} %copy-done.15, bf16[240,3328]{1,0:T(8,128)(2,1)S(1)} %shard_map.76.left_ref, bf16[3328,8192]{1,0:T(8,128)(2,1)} %refs_1_.19), custom_call_target="tpu_custom_call" | custom-call | flops 3271557120 | bytes 15228928 | tf_op jit(solution)/shard_map/pallas_call | solution.py:143
  151.9 2.4 collective-permute-start.20
  154.4 1.5 collective-permute-done.20
  156.4 10.7 %shard_map.80 = (f32[240,1024]{1,0:T(8,128)S(1)}, bf16[240,1024]{1,0:T(8,128)(2,1)S(1)}) custom-call(s32[4]{0:T(128)S(1)} %copy-done.13, bf16[240,3328]{1,0:T(8,128)(2,1)S(1)} %shard_map.76.left_ref, bf16[3328,8192]{1,0:T(8,128)(2,1)} %refs_1_.19), custom_call_target="tpu_custom_call" | custom-call | flops 3271557120 | bytes 15228928 | tf_op jit(solution)/shard_map/pallas_call | solution.py:143
  167.1 1.7 collective-permute-start.22
  168.8 1.5 collective-permute-done.22
  170.8 5.9 %shard_map.81 = f32[240,1024]{1,0:T(8,128)S(1)} custom-call(s32[2]{0:T(128)S(1)} %copy-done.25, bf16[240,3328]{1,0:T(8,128)(2,1)S(1)} %shard_map.76.left_ref, bf16[3328,8192]{1,0:T(8,128)(2,1)} %refs_1_.19), custom_call_target="tpu_custom_call" | custom-call | flops 1635778560 | bytes 8413184 | tf_op jit(solution)/shard_map/pallas_call | solution.py:143
  176.7 1.8 collective-permute-done.24
  178.7 1.3 collective-permute-start.25
  180.0 2.2 collective-permute-done.25
  182.3 1.1 fusion.13
  183.7 6.8 %shard_map.82 = (f32[3328,240]{1,0:T(8,128)S(1)}, f32[1,240,240]{2,1,0:T(8,128)S(1)}) custom-call(s32[2]{0:T(128)S(1)} %copy-done.11, bf16[3328,8192]{1,0:T(8,128)(2,1)} %refs_1_.19, bf16[240,1024]{1,0:T(8,128)(2,1)S(1)} %get-tuple-element.119.refs_2_), custom_call_target="tpu_custom_call" | custom-call | flops 1635778560 | bytes 13205504 | tf_op jit(solution)/shard_map/pallas_call | solution.py:337
  191.4 1.2 collective-permute-start.27
  193.0 1.1 collective-permute-done.27.refs_3_
  194.1 12.0 %shard_map.83 = (f32[3328,240]{1,0:T(8,128)S(1)}, f32[2,240,240]{2,1,0:T(8,128)S(1)}) custom-call(s32[4]{0:T(128)S(1)} %copy-done.23, bf16[3328,8192]{1,0:T(8,128)(2,1)} %refs_1_.19, bf16[240,1024]{1,0:T(8,128)(2,1)S(1)} %collective-permute-done.26.refs_2_, bf16[240,1024]{1,0:T(8,128)(2,1)S(1)} %collective-permute-done.27.refs_3_, ...), custom_call_target="tpu_custom_call", output_to_operand_aliasing={{0}: (4, {})} | custom-call | flops 3271557120 | bytes 20021248 | tf_op jit(solution)/shard_map/pallas_call | solution.py:337
  207.0 1.1 collective-permute-done.29.refs_3_
  208.1 12.0 %shard_map.84 = (f32[3328,240]{1,0:T(8,128)S(1)}, f32[2,240,240]{2,1,0:T(8,128)S(1)}) custom-call(s32[4]{0:T(128)S(1)} %copy-done.21, bf16[3328,8192]{1,0:T(8,128)(2,1)} %refs_1_.19, bf16[240,1024]{1,0:T(8,128)(2,1)S(1)} %collective-permute-done.28.refs_2_, bf16[240,1024]{1,0:T(8,128)(2,1)S(1)} %collective-permute-done.29.refs_3_, ...), custom_call_target="tpu_custom_call", output_to_operand_aliasing={{0}: (4, {})} | custom-call | flops 3271557120 | bytes 20021248 | tf_op jit(solution)/shard_map/pallas_call | solution.py:337
  221.7 1.0 slice.149
  223.1 12.3 %shard_map.85 = (f32[3328,240]{1,0:T(8,128)S(1)}, f32[2,240,240]{2,1,0:T(8,128)S(1)}) custom-call(s32[4]{0:T(128)S(1)} %get-tuple-element.127.refs_0_, bf16[3328,8192]{1,0:T(8,128)(2,1)} %refs_1_.19, bf16[240,1024]{1,0:T(8,128)(2,1)} %collective-permute-done.30.refs_2_, ...), custom_call_target="tpu_custom_call", output_to_operand_aliasing={{0}: (4, {})} | custom-call | flops 3271557120 | bytes 20021248 | tf_op jit(solution)/shard_map/pallas_call | solution.py:337
  236.8 1.3 collective-permute-done.33.refs_3_
  238.1 7.1 %shard_map.86 = (f32[3328,240]{1,0:T(8,128)S(1)}, f32[1,240,240]{2,1,0:T(8,128)S(1)}) custom-call(s32[2]{0:T(128)S(1)} %get-tuple-element.133.refs_0_, bf16[3328,8192]{1,0:T(8,128)(2,1)} %refs_1_.19, bf16[240,512]{1,0:T(8,128)(2,1)} %collective-permute-done.32.refs_2_, ...), custom_call_target="tpu_custom_call", output_to_operand_aliasing={{0}: (4, {})} | custom-call | flops 1635778560 | bytes 13205504 | tf_op jit(solution)/shard_map/pallas_call | solution.py:337
  246.5 1.0 collective-permute-done.34
  247.4 1.2 collective-permute-start.35
  248.6 3.4 %collective-permute-done.35 = f32[120,240]{1,0:T(8,128)S(1)} collective-permute-done((f32[120,240]{1,0:T(8,128)S(1)}, f32[120,240]{1,0:T(8,128)S(1)}, u32[]{:S(2)}, u32[]{:S(2)}) %collective-permute-start.35) | collective-permute-done | bytes 115232 | tf_op jit(solution)/shard_map/ppermute | solution.py:408
  252.1 1.4 collective-permute-start.36
  253.5 22.3 %shard_map.87 = f32[240,240]{1,0:T(8,128)S(1)} custom-call(s32[8]{0:T(128)S(1)} %slice_bitcast_fusion.order_ref, f32[1,240,240]{2,1,0:T(8,128)S(1)} %copy-done.9, f32[2,240,240]{2,1,0:T(8,128)S(1)} %copy-done.3, f32[2,240,240]{2,1,0:T(8,128)S(1)} %copy-done.5, f32[2,240,240]{2,1,0:T(8,128)S(1)} %copy-done.7, f32[1,240,240]{2,1,0:T(8,128)S(1)} %get-tuple-element.117.refs_4_), custom_call_target="tpu_custom_call" | custom-call | tf_op jit(solution)/shard_map/pallas_call | solution.py:235
  277.1 7.0 %collective-permute-done.37 = f32[120,240]{1,0:T(8,128)S(1)} collective-permute-done((f32[120,240]{1,0:T(8,128)S(1)}, f32[120,240]{1,0:T(8,128)S(1)}, u32[]{:S(2)}, u32[]{:S(2)}) %collective-permute-start.37) | collective-permute-done | bytes 115232 | tf_op jit(solution)/shard_map/ppermute | solution.py:408
  284.2 1.0 collective-permute-start.38
  285.2 1.4 convolution_multiply_fusion
  286.6 1.3 fusion.7
  288.6 5.4 %fusion = bf16[3328,224]{0,1:T(8,128)(2,1)} fusion(f32[3328,240]{1,0:T(8,128)S(1)} %get-tuple-element.118, f32[240,224]{0,1:T(8,128)} %copy-done.26, f32[]{:T(128)} %sqrt.3), kind=kOutput, calls=%fused_computation.1 | convolution fusion | flops 2148450304 | bytes 4900868 | tf_op jit(solution)/shard_map/dot_general | solution.py:439
  (142 shorter events, 16.7 us)
Async XLA Ops:
  1.3 6.2 %copy-start.28 = (s32[1,40]{1,0:T(1,128)}, s32[1,40]{1,0:T(1,128)S(1)}, u32[]{:S(2)}) copy-start(s32[1,40]{1,0:T(1,128)S(1)} %constant_dynamic-slice_fusion) | copy-start | bytes 484
  1.4 6.0 %copy-start.18 = (s32[2]{0:T(128)}, s32[2]{0:T(128)S(1)}, u32[]{:S(2)}) copy-start(s32[2]{0:T(128)S(1)} %get-tuple-element.135.ids_ref) | copy-start | bytes 28
  1.4 47.0 %copy-start.24 = (s32[2]{0:T(128)}, s32[2]{0:T(128)S(1)}, u32[]{:S(2)}) copy-start(s32[2]{0:T(128)S(1)} %get-tuple-element.136.ids_ref) | copy-start | bytes 28
  1.4 58.9 %copy-start.10 = (s32[2]{0:T(128)}, s32[2]{0:T(128)S(1)}, u32[]{:S(2)}) copy-start(s32[2]{0:T(128)S(1)} %get-tuple-element.134.refs_0_) | copy-start | bytes 28
  7.5 1.6 collective-permute-start
  7.6 9.4 %copy-start.16 = (s32[4]{0:T(128)}, s32[4]{0:T(128)S(1)}, u32[]{:S(2)}) copy-start(s32[4]{0:T(128)S(1)} %get-tuple-element.130.ids_ref) | copy-start | bytes 52
  7.7 17.7 %copy-start.14 = (s32[4]{0:T(128)}, s32[4]{0:T(128)S(1)}, u32[]{:S(2)}) copy-start(s32[4]{0:T(128)S(1)} %get-tuple-element.131.ids_ref) | copy-start | bytes 52
  7.7 29.2 %copy-start.12 = (s32[4]{0:T(128)}, s32[4]{0:T(128)S(1)}, u32[]{:S(2)}) copy-start(s32[4]{0:T(128)S(1)} %get-tuple-element.132.ids_ref) | copy-start | bytes 52
  7.7 63.2 %copy-start.22 = (s32[4]{0:T(128)}, s32[4]{0:T(128)S(1)}, u32[]{:S(2)}) copy-start(s32[4]{0:T(128)S(1)} %get-tuple-element.129.refs_0_) | copy-start | bytes 52
  7.7 76.4 %copy-start.20 = (s32[4]{0:T(128)}, s32[4]{0:T(128)S(1)}, u32[]{:S(2)}) copy-start(s32[4]{0:T(128)S(1)} %get-tuple-element.128.refs_0_) | copy-start | bytes 52
  17.0 2.8 collective-permute-start.1
  17.2 6.5 %collective-permute-start.2 = (bf16[240,512]{1,0:T(8,128)(2,1)S(1)}, bf16[240,512]{1,0:T(8,128)(2,1)S(1)}, u32[]{:S(2)}, u32[]{:S(2)}) collective-permute-start(bf16[240,512]{1,0:T(8,128)(2,1)S(1)} %add_convert_fusion.5), channel_id=1, source_target_pairs={{0,4},{1,3},{4,8},{5,1},{8,12},{9,5},{12,14},{13,9},{14,10},{15,13... | collective-permute-start | bytes 737288 | tf_op jit(solution)/shard_map/ppermute | solution.py:374
  23.9 10.8 %collective-permute-start.4 = (bf16[240,1024]{1,0:T(8,128)(2,1)S(1)}, bf16[240,1024]{1,0:T(8,128)(2,1)S(1)}, u32[]{:S(2)}, u32[]{:S(2)}) collective-permute-start(bf16[240,1024]{1,0:T(8,128)(2,1)S(1)} %pad_maximum_fusion), channel_id=1, source_target_pairs={{0,4},{1,3},{4,8},{5,1},{8,12},{9,5},{12,14},{13,9},{14,10},{15,13... | collective-permute-start | bytes 1474568 | tf_op jit(solution)/shard_map/ppermute | solution.py:374
  33.3 2.9 collective-permute-start.3
  36.4 10.0 %collective-permute-start.6 = (bf16[240,1024]{1,0:T(8,128)(2,1)S(1)}, bf16[240,1024]{1,0:T(8,128)(2,1)S(1)}, u32[]{:S(2)}, u32[]{:S(2)}) collective-permute-start(bf16[240,1024]{1,0:T(8,128)(2,1)S(1)} %add_convert_fusion.3), channel_id=1, source_target_pairs={{0,4},{1,3},{4,8},{5,1},{8,12},{9,5},{12,14},{13,9},{14,10},{15,13... | collective-permute-start | bytes 1474568 | tf_op jit(solution)/shard_map/ppermute | solution.py:374
  44.8 3.2 %collective-permute-start.5 = (bf16[240,1024]{1,0:T(8,128)(2,1)S(1)}, bf16[240,1024]{1,0:T(8,128)(2,1)S(1)}, u32[]{:S(2)}, u32[]{:S(2)}) collective-permute-start(bf16[240,1024]{1,0:T(8,128)(2,1)S(1)} %get-tuple-element.73), channel_id=1, source_target_pairs={{0,1},{1,0},{2,3},{3,2},{4,5},{5,4},{6,7},{7,6},{8,9},{9,8},{10,11... | collective-permute-start | bytes 1474568 | tf_op jit(solution)/shard_map/ppermute | solution.py:365
  48.2 8.0 %collective-permute-start.7 = (bf16[240,1024]{1,0:T(8,128)(2,1)S(1)}, bf16[240,1024]{1,0:T(8,128)(2,1)S(1)}, u32[]{:S(2)}, u32[]{:S(2)}) collective-permute-start(bf16[240,1024]{1,0:T(8,128)(2,1)S(1)} %add_convert_fusion.2), channel_id=1, source_target_pairs={{0,4},{1,3},{4,8},{5,1},{8,12},{9,5},{12,14},{13,9},{14,10},{15,13... | collective-permute-start | bytes 1474568 | tf_op jit(solution)/shard_map/ppermute | solution.py:374
  56.4 3.5 %collective-permute-start.8 = (f32[240,1024]{1,0:T(8,128)S(1)}, f32[240,1024]{1,0:T(8,128)S(1)}, u32[]{:S(2)}, u32[]{:S(2)}) collective-permute-start(f32[240,1024]{1,0:T(8,128)S(1)} %convert_add_fusion.2), channel_id=1, source_target_pairs={{0,1},{1,0},{2,3},{3,2},{4,5},{5,4},{6,7},{7,6},{8,9},{9,8},{10,11... | collective-permute-start | bytes 2949128 | tf_op jit(solution)/shard_map/ppermute | solution.py:377
  60.1 8.0 %collective-permute-start.9 = (bf16[240,1024]{1,0:T(8,128)(2,1)S(1)}, bf16[240,1024]{1,0:T(8,128)(2,1)S(1)}, u32[]{:S(2)}, u32[]{:S(2)}) collective-permute-start(bf16[240,1024]{1,0:T(8,128)(2,1)S(1)} %fusion.3.refs_2_), channel_id=1, source_target_pairs={{0,4},{1,3},{4,8},{5,1},{8,12},{9,5},{12,14},{13,9},{14,10},{15,13... | collective-permute-start | bytes 1474568 | tf_op jit(solution)/shard_map/ppermute | solution.py:388
  68.1 2.7 collective-permute-start.11
  69.3 12.8 %collective-permute-start.10 = (bf16[240,1024]{1,0:T(8,128)(2,1)S(1)}, bf16[240,1024]{1,0:T(8,128)(2,1)S(1)}, u32[]{:S(2)}, u32[]{:S(2)}) collective-permute-start(bf16[240,1024]{1,0:T(8,128)(2,1)S(1)} %collective-permute-done.9.refs_2_), channel_id=1, source_target_pairs={{0,4},{1,3},{4,8},{5,1},{8,12},{9,5},{12,14},{13,9},{14,10},{15,13... | collective-permute-start | bytes 1474568 | tf_op jit(solution)/shard_map/ppermute | solution.py:388
  82.1 1.9 collective-permute-start.13
  82.6 12.8 %collective-permute-start.12 = (bf16[240,1024]{1,0:T(8,128)(2,1)S(1)}, bf16[240,1024]{1,0:T(8,128)(2,1)S(1)}, u32[]{:S(2)}, u32[]{:S(2)}) collective-permute-start(bf16[240,1024]{1,0:T(8,128)(2,1)S(1)} %collective-permute-done.10.refs_2_), channel_id=1, source_target_pairs={{0,4},{1,3},{4,8},{5,1},{8,12},{9,5},{12,14},{13,9},{14,10},{15,13... | collective-permute-start | bytes 1474568 | tf_op jit(solution)/shard_map/ppermute | solution.py:388
  95.3 1.9 collective-permute-start.15
  95.8 12.8 %collective-permute-start.14 = (bf16[240,512]{1,0:T(8,128)(2,1)S(1)}, bf16[240,512]{1,0:T(8,128)(2,1)S(1)}, u32[]{:S(2)}, u32[]{:S(2)}) collective-permute-start(bf16[240,512]{1,0:T(8,128)(2,1)S(1)} %slice.139), channel_id=1, source_target_pairs={{0,4},{1,3},{4,8},{5,1},{8,12},{9,5},{12,14},{13,9},{14,10},{15,13... | collective-permute-start | bytes 737288 | tf_op jit(solution)/shard_map/ppermute | solution.py:388
  108.6 1.7 collective-permute-start.16
  110.2 6.5 %copy-start.19 = (s32[2]{0:T(128)S(1)}, s32[2]{0:T(128)}, u32[]{:S(2)}) copy-start(s32[2]{0:T(128)} %copy-done.18) | copy-start | bytes 28
  116.8 7.5 %copy-start.17 = (s32[4]{0:T(128)S(1)}, s32[4]{0:T(128)}, u32[]{:S(2)}) copy-start(s32[4]{0:T(128)} %copy-done.16) | copy-start | bytes 52
  122.6 1.6 collective-permute-start.17
  135.0 6.2 %copy-start.15 = (s32[4]{0:T(128)S(1)}, s32[4]{0:T(128)}, u32[]{:S(2)}) copy-start(s32[4]{0:T(128)} %copy-done.14) | copy-start | bytes 52
  135.1 1.9 collective-permute-start.18
  135.5 5.3 %collective-permute-start.19 = (bf16[240,512]{1,0:T(8,128)(2,1)S(1)}, bf16[240,512]{1,0:T(8,128)(2,1)S(1)}, u32[]{:S(2)}, u32[]{:S(2)}) collective-permute-start(bf16[240,512]{1,0:T(8,128)(2,1)S(1)} %add_convert_fusion.4), channel_id=1, source_target_pairs={{0,4},{1,3},{4,8},{5,1},{8,12},{9,5},{12,14},{13,9},{14,10},{15,13... | collective-permute-start | bytes 737288 | tf_op jit(solution)/shard_map/ppermute | solution.py:374
  141.0 15.4 %copy-start.13 = (s32[4]{0:T(128)S(1)}, s32[4]{0:T(128)}, u32[]{:S(2)}) copy-start(s32[4]{0:T(128)} %copy-done.12) | copy-start | bytes 52
  141.0 13.4 %collective-permute-start.21 = (bf16[240,1024]{1,0:T(8,128)(2,1)S(1)}, bf16[240,1024]{1,0:T(8,128)(2,1)S(1)}, u32[]{:S(2)}, u32[]{:S(2)}) collective-permute-start(bf16[240,1024]{1,0:T(8,128)(2,1)S(1)} %pad_maximum_fusion.1), channel_id=1, source_target_pairs={{0,4},{1,3},{4,8},{5,1},{8,12},{9,5},{12,14},{13,9},{14,10},{15,13... | collective-permute-start | bytes 1474568 | tf_op jit(solution)/shard_map/ppermute | solution.py:374
  151.9 3.9 %collective-permute-start.20 = (bf16[240,1024]{1,0:T(8,128)(2,1)S(1)}, bf16[240,1024]{1,0:T(8,128)(2,1)S(1)}, u32[]{:S(2)}, u32[]{:S(2)}) collective-permute-start(bf16[240,1024]{1,0:T(8,128)(2,1)S(1)} %get-tuple-element.93), channel_id=1, source_target_pairs={{0,1},{1,0},{2,3},{3,2},{4,5},{5,4},{6,7},{7,6},{8,9},{9,8},{10,11... | collective-permute-start | bytes 1474568 | tf_op jit(solution)/shard_map/ppermute | solution.py:365
  156.1 14.8 %copy-start.25 = (s32[2]{0:T(128)S(1)}, s32[2]{0:T(128)}, u32[]{:S(2)}) copy-start(s32[2]{0:T(128)} %copy-done.24) | copy-start | bytes 28
  156.1 12.7 %collective-permute-start.23 = (bf16[240,1024]{1,0:T(8,128)(2,1)S(1)}, bf16[240,1024]{1,0:T(8,128)(2,1)S(1)}, u32[]{:S(2)}, u32[]{:S(2)}) collective-permute-start(bf16[240,1024]{1,0:T(8,128)(2,1)S(1)} %add_convert_fusion.1), channel_id=1, source_target_pairs={{0,4},{1,3},{4,8},{5,1},{8,12},{9,5},{12,14},{13,9},{14,10},{15,13... | collective-permute-start | bytes 1474568 | tf_op jit(solution)/shard_map/ppermute | solution.py:374
  167.1 3.2 %collective-permute-start.22 = (bf16[240,1024]{1,0:T(8,128)(2,1)S(1)}, bf16[240,1024]{1,0:T(8,128)(2,1)S(1)}, u32[]{:S(2)}, u32[]{:S(2)}) collective-permute-start(bf16[240,1024]{1,0:T(8,128)(2,1)S(1)} %get-tuple-element.97), channel_id=1, source_target_pairs={{0,1},{1,0},{2,3},{3,2},{4,5},{5,4},{6,7},{7,6},{8,9},{9,8},{10,11... | collective-permute-start | bytes 1474568 | tf_op jit(solution)/shard_map/ppermute | solution.py:365
  170.5 8.0 %collective-permute-start.24 = (bf16[240,1024]{1,0:T(8,128)(2,1)S(1)}, bf16[240,1024]{1,0:T(8,128)(2,1)S(1)}, u32[]{:S(2)}, u32[]{:S(2)}) collective-permute-start(bf16[240,1024]{1,0:T(8,128)(2,1)S(1)} %add_convert_fusion), channel_id=1, source_target_pairs={{0,4},{1,3},{4,8},{5,1},{8,12},{9,5},{12,14},{13,9},{14,10},{15,13... | collective-permute-start | bytes 1474568 | tf_op jit(solution)/shard_map/ppermute | solution.py:374
  178.7 3.5 %collective-permute-start.25 = (f32[240,1024]{1,0:T(8,128)S(1)}, f32[240,1024]{1,0:T(8,128)S(1)}, u32[]{:S(2)}, u32[]{:S(2)}) collective-permute-start(f32[240,1024]{1,0:T(8,128)S(1)} %convert_add_fusion), channel_id=1, source_target_pairs={{0,1},{1,0},{2,3},{3,2},{4,5},{5,4},{6,7},{7,6},{8,9},{9,8},{10,11... | collective-permute-start | bytes 2949128 | tf_op jit(solution)/shard_map/ppermute | solution.py:377
  183.4 10.7 %copy-start.23 = (s32[4]{0:T(128)S(1)}, s32[4]{0:T(128)}, u32[]{:S(2)}) copy-start(s32[4]{0:T(128)} %copy-done.22) | copy-start | bytes 52
  183.4 8.0 %collective-permute-start.26 = (bf16[240,1024]{1,0:T(8,128)(2,1)S(1)}, bf16[240,1024]{1,0:T(8,128)(2,1)S(1)}, u32[]{:S(2)}, u32[]{:S(2)}) collective-permute-start(bf16[240,1024]{1,0:T(8,128)(2,1)S(1)} %get-tuple-element.119.refs_2_), channel_id=1, source_target_pairs={{0,4},{1,3},{4,8},{5,1},{8,12},{9,5},{12,14},{13,9},{14,10},{15,13... | collective-permute-start | bytes 1474568 | tf_op jit(solution)/shard_map/ppermute | solution.py:388
  191.4 16.7 %copy-start.21 = (s32[4]{0:T(128)S(1)}, s32[4]{0:T(128)}, u32[]{:S(2)}) copy-start(s32[4]{0:T(128)} %copy-done.20) | copy-start | bytes 52
  191.4 2.7 collective-permute-start.27
  192.6 13.5 %collective-permute-start.28 = (bf16[240,1024]{1,0:T(8,128)(2,1)S(1)}, bf16[240,1024]{1,0:T(8,128)(2,1)S(1)}, u32[]{:S(2)}, u32[]{:S(2)}) collective-permute-start(bf16[240,1024]{1,0:T(8,128)(2,1)S(1)} %collective-permute-done.26.refs_2_), channel_id=1, source_target_pairs={{0,4},{1,3},{4,8},{5,1},{8,12},{9,5},{12,14},{13,9},{14,10},{15,13... | collective-permute-start | bytes 1474568 | tf_op jit(solution)/shard_map/ppermute | solution.py:388
  206.1 14.0 %copy-start.2 = (f32[2,240,240]{2,1,0:T(8,128)}, f32[2,240,240]{2,1,0:T(8,128)S(1)}, u32[]{:S(2)}) copy-start(f32[2,240,240]{2,1,0:T(8,128)S(1)} %get-tuple-element.105.refs_1_) | copy-start | bytes 1382404
  206.1 15.2 %copy-start.30 = (s32[240]{0:T(256)S(1)}, s32[240]{0:T(256)}, u32[]{:S(2)}) copy-start(s32[240]{0:T(256)} %param.6) | copy-start | bytes 2884
  206.2 1.9 collective-permute-start.29
  206.6 14.3 %collective-permute-start.30 = (bf16[240,1024]{1,0:T(8,128)(2,1)S(1)}, bf16[240,1024]{1,0:T(8,128)(2,1)}, u32[]{:S(2)}, u32[]{:S(2)}) collective-permute-start(bf16[240,1024]{1,0:T(8,128)(2,1)S(1)} %collective-permute-done.28.refs_2_), channel_id=1, source_target_pairs={{0,4},{1,3},{4,8},{5,1},{8,12},{9,5},{12,14},{13,9},{14,10},{15,13... | collective-permute-start | bytes 1474568 | tf_op jit(solution)/shard_map/ppermute | solution.py:388
  220.9 2.2 collective-permute-start.31
  222.7 13.6 %collective-permute-start.32 = (bf16[240,512]{1,0:T(8,128)(2,1)S(1)}, bf16[240,512]{1,0:T(8,128)(2,1)}, u32[]{:S(2)}, u32[]{:S(2)}) collective-permute-start(bf16[240,512]{1,0:T(8,128)(2,1)S(1)} %slice.149), channel_id=1, source_target_pairs={{0,4},{1,3},{4,8},{5,1},{8,12},{9,5},{12,14},{13,9},{14,10},{15,13... | collective-permute-start | bytes 737288 | tf_op jit(solution)/shard_map/ppermute | solution.py:388
  236.3 1.9 collective-permute-start.33
  245.3 8.2 %copy-start.29 = (s32[1,40]{1,0:T(1,128)S(1)}, s32[1,40]{1,0:T(1,128)}, u32[]{:S(2)}) copy-start(s32[1,40]{1,0:T(1,128)} %copy-done.28) | copy-start | bytes 484
  245.3 8.2 %copy-start.3 = (f32[2,240,240]{2,1,0:T(8,128)S(1)}, f32[2,240,240]{2,1,0:T(8,128)}, u32[]{:S(2)}) copy-start(f32[2,240,240]{2,1,0:T(8,128)} %copy-done.2) | copy-start | bytes 1382404
  245.3 8.2 %copy-start.5 = (f32[2,240,240]{2,1,0:T(8,128)S(1)}, f32[2,240,240]{2,1,0:T(8,128)}, u32[]{:S(2)}) copy-start(f32[2,240,240]{2,1,0:T(8,128)} %copy-done.4) | copy-start | bytes 1382404
  245.3 8.2 %copy-start.7 = (f32[2,240,240]{2,1,0:T(8,128)S(1)}, f32[2,240,240]{2,1,0:T(8,128)}, u32[]{:S(2)}) copy-start(f32[2,240,240]{2,1,0:T(8,128)} %copy-done.6) | copy-start | bytes 1382404
  245.3 8.2 %copy-start.9 = (f32[1,240,240]{2,1,0:T(8,128)S(1)}, f32[1,240,240]{2,1,0:T(8,128)}, u32[]{:S(2)}) copy-start(f32[1,240,240]{2,1,0:T(8,128)} %copy-done.8) | copy-start | bytes 691204
  246.0 39.2 %copy-start.27 = (f32[240,1024]{1,0:T(8,128)S(1)}, f32[240,1024]{1,0:T(8,128)}, u32[]{:S(2)}) copy-start(f32[240,1024]{1,0:T(8,128)} %get-tuple-element.120) | copy-start | bytes 2949124
  246.0 1.4 collective-permute-start.34
  247.4 4.6 %collective-permute-start.35 = (f32[120,240]{1,0:T(8,128)S(1)}, f32[120,240]{1,0:T(8,128)S(1)}, u32[]{:S(2)}, u32[]{:S(2)}) collective-permute-start(f32[120,240]{1,0:T(8,128)S(1)} %select_add_fusion), channel_id=1, source_target_pairs={{0,2},{1,3},{2,0},{3,1},{4,6},{5,7},{6,4},{7,5},{8,10},{9,11},{10,... | collective-permute-start | bytes 345608 | tf_op jit(solution)/shard_map/ppermute | solution.py:408
  252.1 23.8 %collective-permute-start.36 = (f32[120,240]{1,0:T(8,128)S(1)}, f32[120,240]{1,0:T(8,128)S(1)}, u32[]{:S(2)}, u32[]{:S(2)}) collective-permute-start(f32[120,240]{1,0:T(8,128)S(1)} %add.101), channel_id=1, source_target_pairs={{0,4},{1,5},{2,6},{3,7},{4,0},{5,1},{6,2},{7,3},{8,12},{9,13},{10,... | collective-permute-start | bytes 345608 | tf_op jit(solution)/shard_map/ppermute | solution.py:408
  275.9 8.3 %collective-permute-start.37 = (f32[120,240]{1,0:T(8,128)S(1)}, f32[120,240]{1,0:T(8,128)S(1)}, u32[]{:S(2)}, u32[]{:S(2)}) collective-permute-start(f32[120,240]{1,0:T(8,128)S(1)} %add.102), channel_id=1, source_target_pairs={{0,8},{1,9},{2,10},{3,11},{4,12},{5,13},{6,14},{7,15},{8,0},{9,1},... | collective-permute-start | bytes 345608 | tf_op jit(solution)/shard_map/ppermute | solution.py:408
  277.1 9.5 %copy-start.26 = (f32[240,224]{0,1:T(8,128)}, f32[240,224]{0,1:T(8,128)S(1)}, u32[]{:S(2)}) copy-start(f32[240,224]{0,1:T(8,128)S(1)} %fusion.9) | copy-start | bytes 645124
  284.2 2.4 collective-permute-start.38
  (6 other events, 12.3 us)
